TPU v7x, 512 devices: a whole 4x8x8 slice. The times are simulated.
512 devices in a mesh: blk: 64 (over z_hi, y, core), head: 8 (over x, z_lo).
Axes of the slice: x: 4, y: 8, z: 8 (z_hi: 4, z_lo: 2; z = z_hi * 2 + z_lo), core: 2. Of those that a mesh axis runs over, the one named last changes fastest.
Arguments:
- queries: bfloat16 [65536, 2048], P(('blk', 'head')), may hold values from -20 to 20
- keys: bfloat16 [65536, 1024], P(('blk', 'head')), may hold values from -20 to 20
- values: bfloat16 [65536, 1024], P(('blk', 'head')), may hold values from -6 to 6
- outputs: bfloat16 [65536, 2048], P(('blk', 'head')), may hold values from -6 to 6
- out_grads: bfloat16 [65536, 2048], P(('blk', 'head')), may hold values from -6 to 6
- segment_ids: int32 [65536], replicated, may hold values from 0 to 255, never falling along the last dimension, each value on 1 to 512 neighbouring positions
- block_order: int32 [128], replicated, may hold values from 0 to 127, as said below
Outputs:
- query_grads: bfloat16 [65536, 2048], P(('blk', 'head'))
- key_grads: bfloat16 [65536, 1024], P(('blk', 'head'))
- value_grads: bfloat16 [65536, 1024], P(('blk', 'head'))
Inputs may be any that keep to these rules, and one draw needn't show every extreme that they name: `segment_ids`: never falling along the sequence; each document has 1 to 512 tokens, one exactly 512. `block_order`: slots 2 i and 2 i + 1 hold the half-blocks i and 127 - i, in either order.
All inputs are finite; a program needn't handle non-finite values.
Results may differ from a plain program's by a relative error of at most 0.008.
Values may be sent and summed in bfloat16 or wider, within the bound.
A program may use at most 64 MiB of HBM per device.

v0:
```python
import jax
import jax.numpy as jnp
from jax import lax
from jax.sharding import PartitionSpec as P

HEAD_SIZE = 128


NEGATIVE = -1e30


def shifted(value, axis, steps):
    count = lax.axis_size(axis)
    initial, last = (max(0, -steps), min(count, count - steps))
    return lax.ppermute(value, axis, [(source, source + steps) for source in range(initial, last)])


def row_terms_of(output_rows, grad_rows, head_dim):
    count_rows = output_rows.shape[0]
    heads = output_rows.shape[1] // head_dim
    product = output_rows.astype(jnp.float32) * grad_rows.astype(jnp.float32)
    return jnp.sum(product.reshape(count_rows, heads, head_dim), axis=2)


def local(queries, keys, values, outputs, out_grads, segment_ids, block_order):
    cycle_size = lax.axis_size("blk")
    cycle_index = lax.axis_index("blk")
    query_rows, key_rows, value_rows, output_rows, grad_rows = (
        lax.all_to_all(queries, "head", split_axis=1, concat_axis=0, tiled=True),
        lax.all_to_all(keys, "head", split_axis=1, concat_axis=0, tiled=True),
        lax.all_to_all(values, "head", split_axis=1, concat_axis=0, tiled=True),
        lax.all_to_all(outputs, "head", split_axis=1, concat_axis=0, tiled=True),
        lax.all_to_all(out_grads, "head", split_axis=1, concat_axis=0, tiled=True),
    )
    row_delta = row_terms_of(output_rows, grad_rows, HEAD_SIZE)
    block_rows = query_rows.shape[0]
    half_rows = block_rows // 2
    q_local = query_rows.shape[1] // HEAD_SIZE
    kv_local = key_rows.shape[1] // HEAD_SIZE
    query_group_size = q_local // kv_local
    softmax_scale = HEAD_SIZE ** (-0.5)
    row_offsets = jnp.arange(half_rows, dtype=jnp.int32)

    def half_of(source, late):
        clamped = jnp.clip(source, 0, cycle_size - 1)
        slots = lax.dynamic_slice_in_dim(block_order, 2 * clamped, 2)
        early_slot = (slots[0] > slots[1]).astype(jnp.int32)
        slot = 1 - early_slot if late else early_slot
        which = jnp.where(slot == 0, slots[0], slots[1])
        positions = which * half_rows + row_offsets
        return (slot, positions, segment_ids[positions])

    def rows_at(array, slot):
        return lax.dynamic_slice_in_dim(array, slot * half_rows, half_rows, 0)

    def place_half(term, slot):
        empty = jnp.zeros((block_rows, term.shape[1]), term.dtype)
        return lax.dynamic_update_slice_in_dim(empty, term, slot * half_rows, 0)

    own_half = {False: half_of(cycle_index, False), True: half_of(cycle_index, True)}
    early_slot = own_half[False][0]
    query_half = {}
    grad_half = {}
    delta_half = {}
    for late in (False, True):
        slot = own_half[late][0]
        query_half[late] = rows_at(query_rows, slot).reshape(
            half_rows, kv_local, query_group_size, HEAD_SIZE
        )
        grad_half[late] = rows_at(grad_rows, slot).reshape(
            half_rows, kv_local, query_group_size, HEAD_SIZE
        )
        delta_half[late] = rows_at(row_delta, slot).T.reshape(kv_local, query_group_size, half_rows)
    neighbour = {}
    for offset, late in ((1, False), (-1, True)):
        moved = shifted((key_rows, value_rows), "blk", offset)
        source_slot = half_of(cycle_index - offset, late)[0]
        neighbour[offset] = (rows_at(moved[0], source_slot), rows_at(moved[1], source_slot))
    specs = [
        (0, False, False),
        (0, True, True),
        (0, True, False),
        (1, False, False),
        (-1, True, True),
    ]
    blocks = {}
    masks = {}
    for spec in specs:
        offset, q_late, k_late = spec
        if offset == 0:
            slot = own_half[k_late][0]
            blocks[spec] = (rows_at(key_rows, slot), rows_at(value_rows, slot))
        else:
            blocks[spec] = neighbour[offset]
        source = cycle_index - offset
        inside = (source >= 0) & (source < cycle_size)
        k_info = half_of(source, k_late)
        q_info = own_half[q_late]
        masks[spec] = (
            (q_info[2][:, None] == k_info[2][None, :])
            & (k_info[1][None, :] <= q_info[1][:, None])
            & inside
        )

    def scores_of(query_four, key_block, visible):
        key_three = key_block.reshape(half_rows, kv_local, HEAD_SIZE)
        raw = (
            jnp.einsum("tjgd,ujd->jgtu", query_four, key_three, preferred_element_type=jnp.float32)
            * softmax_scale
        )
        return jnp.where(visible[None, None], raw, NEGATIVE)

    log_sums = {}
    for late in (False, True):
        stats = (
            jnp.full((kv_local, query_group_size, half_rows), NEGATIVE, jnp.float32),
            jnp.zeros((kv_local, query_group_size, half_rows), jnp.float32),
        )
        for spec in specs:
            if spec[1] == late:
                update_visible = masks[spec]
                maxima, totals = stats
                update_scores = scores_of(query_half[late], blocks[spec][0], update_visible)
                new_max = jnp.maximum(maxima, jnp.max(update_scores, axis=3))
                update_terms = jnp.where(
                    update_visible[None, None], jnp.exp(update_scores - new_max[..., None]), 0.0
                )
                stats = (
                    new_max,
                    totals * jnp.exp(maxima - new_max) + jnp.sum(update_terms, axis=3),
                )
        log_sums[late] = stats[0] + jnp.log(stats[1])
    terms = {}
    for spec in specs:
        tile_q_late = spec[1]
        tile_key_block = blocks[spec][0]
        tile_visible = masks[spec]
        tile_query_four = query_half[tile_q_late]
        grad_four = grad_half[tile_q_late]
        tile_key_three = tile_key_block.reshape(half_rows, kv_local, HEAD_SIZE)
        value_three = blocks[spec][1].reshape(half_rows, kv_local, HEAD_SIZE)
        scores = scores_of(tile_query_four, tile_key_block, tile_visible)
        weights = jnp.where(
            tile_visible[None, None], jnp.exp(scores - log_sums[tile_q_late][..., None]), 0.0
        )
        weights_b = weights.astype(jnp.bfloat16)
        value_term = jnp.einsum(
            "jgtu,tjgd->ujd", weights_b, grad_four, preferred_element_type=jnp.float32
        )
        weight_grads = jnp.einsum(
            "tjgd,ujd->jgtu", grad_four, value_three, preferred_element_type=jnp.float32
        )
        score_grads = weights * (weight_grads - delta_half[tile_q_late][..., None])
        score_grads_b = score_grads.astype(jnp.bfloat16)
        query_term = jnp.einsum(
            "jgtu,ujd->tjgd", score_grads_b, tile_key_three, preferred_element_type=jnp.float32
        )
        key_term = jnp.einsum(
            "jgtu,tjgd->ujd", score_grads_b, tile_query_four, preferred_element_type=jnp.float32
        )
        terms[spec] = (
            query_term.reshape(half_rows, q_local * HEAD_SIZE),
            key_term.reshape(half_rows, kv_local * HEAD_SIZE),
            value_term.reshape(half_rows, kv_local * HEAD_SIZE),
        )
    query_early = terms[0, False, False][0] + terms[1, False, False][0]
    query_late = terms[0, True, True][0] + terms[0, True, False][0] + terms[-1, True, True][0]
    key_early = terms[0, False, False][1] + terms[0, True, False][1]
    value_early = terms[0, False, False][2] + terms[0, True, False][2]
    key_late = terms[0, True, True][1]
    value_late = terms[0, True, True][2]
    received = {}
    for offset, late in ((1, False), (-1, True)):
        spec = (offset, late, late)
        source_slot = half_of(cycle_index - offset, late)[0]
        back_key, back_value = (
            shifted(
                place_half(terms[spec][1], source_slot).astype(jnp.bfloat16), "blk", -offset
            ).astype(jnp.float32),
            shifted(
                place_half(terms[spec][2], source_slot).astype(jnp.bfloat16), "blk", -offset
            ).astype(jnp.float32),
        )
        slot = own_half[late][0]
        received[late] = (rows_at(back_key, slot), rows_at(back_value, slot))
    key_early = key_early + received[False][0]
    value_early = value_early + received[False][1]
    key_late = key_late + received[True][0]
    value_late = value_late + received[True][1]

    def join(early, late):
        first = jnp.where(early_slot == 0, early, late)
        second = jnp.where(early_slot == 0, late, early)
        return jnp.concatenate([first, second], axis=0)

    query_block_grads = (join(query_early, query_late) * softmax_scale).astype(jnp.bfloat16)
    key_block_grads = (join(key_early, key_late) * softmax_scale).astype(jnp.bfloat16)
    value_block_grads = join(value_early, value_late).astype(jnp.bfloat16)
    return (
        lax.all_to_all(query_block_grads, "head", split_axis=0, concat_axis=1, tiled=True),
        lax.all_to_all(key_block_grads, "head", split_axis=0, concat_axis=1, tiled=True),
        lax.all_to_all(value_block_grads, "head", split_axis=0, concat_axis=1, tiled=True),
    )


def solution(mesh):
    return jax.shard_map(
        local,
        mesh=mesh,
        in_specs=(
            P(("blk", "head"), None),
            P(("blk", "head"), None),
            P(("blk", "head"), None),
            P(("blk", "head"), None),
            P(("blk", "head"), None),
            P(),
            P(),
        ),
        out_specs=(P(("blk", "head"), None), P(("blk", "head"), None), P(("blk", "head"), None)),
        check_vma=False,
    )
```

profile of v0, /device:TPU:256, one launch (start us, length us, event | category | flops | bytes accessed | tf_op | source)
XLA Modules:
  0.0 185.8 jit_solution(12750449529479060714)
XLA Ops:
  2.3 5.2 %all-to-all-start = ((bf16[128,8,128]{2,0,1:T(8,128)(2,1)}), bf16[128,8,128]{2,0,1:T(8,128)(2,1)}, u32[]{:S(2)}, u32[]{:S(2)}) async-start(bf16[128,8,128]{2,0,1:T(8,128)(2,1)} %copy_bitcast_fusion.3), calls=%async_computation | async-start | bytes 524288 | tf_op jit(solution)/shard_map/all_to_all | solution.py:30
  7.5 1.7 copy_bitcast_fusion.2
  9.2 5.7 %all-to-all-done = bf16[128,8,128]{2,0,1:T(8,128)(2,1)} async-done(((bf16[128,8,128]{2,0,1:T(8,128)(2,1)}), bf16[128,8,128]{2,0,1:T(8,128)(2,1)}, u32[]{:S(2)}, u32[]{:S(2)}) %all-to-all-start) | async-done | bytes 262176 | tf_op jit(solution)/shard_map/all_to_all | solution.py:30
  14.9 4.0 %all-to-all-start.2 = ((bf16[128,8,128]{2,0,1:T(8,128)(2,1)}), bf16[128,8,128]{2,0,1:T(8,128)(2,1)}, u32[]{:S(2)}, u32[]{:S(2)}) async-start(bf16[128,8,128]{2,0,1:T(8,128)(2,1)} %copy_bitcast_fusion.2), calls=%async_computation.2 | async-start | bytes 524288 | tf_op jit(solution)/shard_map/all_to_all | solution.py:31
  20.0 6.3 %all-to-all-done.2 = bf16[128,8,128]{2,0,1:T(8,128)(2,1)} async-done(((bf16[128,8,128]{2,0,1:T(8,128)(2,1)}), bf16[128,8,128]{2,0,1:T(8,128)(2,1)}, u32[]{:S(2)}, u32[]{:S(2)}) %all-to-all-start.2) | async-done | bytes 262176 | tf_op jit(solution)/shard_map/all_to_all | solution.py:31
  26.3 3.5 %all-to-all-start.3 = ((bf16[128,8,256]{0,2,1:T(8,128)(2,1)}), bf16[128,8,256]{0,2,1:T(8,128)(2,1)S(1)}, u32[]{:S(2)}, u32[]{:S(2)}) async-start(bf16[128,8,256]{0,2,1:T(8,128)(2,1)} %bitcast.23), calls=%async_computation.3 | async-start | bytes 1048576 | tf_op jit(solution)/shard_map/all_to_all | solution.py:33
  37.2 1.2 all-to-all-done.3
  38.4 4.4 %all-to-all-start.1 = ((bf16[128,8,256]{0,2,1:T(8,128)(2,1)}), bf16[128,8,256]{0,2,1:T(8,128)(2,1)S(1)}, u32[]{:S(2)}, u32[]{:S(2)}) async-start(bf16[128,8,256]{0,2,1:T(8,128)(2,1)} %bitcast.7), calls=%async_computation.1 | async-start | bytes 1048576 | tf_op jit(solution)/shard_map/all_to_all | solution.py:29
  42.9 3.1 %gather_fusion.2 = s32[512]{0:T(512)S(1)} fusion(s32[65536]{0:T(1024)S(1)} %copy-done.1, s32[1024]{0:T(1024)S(1)} %pad_clamp_fusion.1), kind=kCustom, calls=%fused_computation.2 | custom fusion | bytes 6144 | tf_op jit(solution)/shard_map/gather | solution.py:51
  46.0 3.1 %gather_fusion.3 = s32[512]{0:T(512)S(1)} fusion(s32[65536]{0:T(1024)S(1)} %copy-done.1, s32[1024]{0:T(1024)S(1)} %pad_clamp_fusion), kind=kCustom, calls=%fused_computation.3 | custom fusion | bytes 6144 | tf_op jit(solution)/shard_map/gather | solution.py:51
  53.7 3.1 %gather_fusion = s32[512]{0:T(512)S(1)} fusion(s32[65536]{0:T(1024)S(1)} %copy-done.1, s32[1024]{0:T(1024)S(1)} %pad_clamp_fusion.3), kind=kCustom, calls=%fused_computation | custom fusion | bytes 6144 | tf_op jit(solution)/shard_map/gather | solution.py:51
  56.9 3.1 %gather_fusion.1 = s32[512]{0:T(512)S(1)} fusion(s32[65536]{0:T(1024)S(1)} %copy-done.1, s32[1024]{0:T(1024)S(1)} %pad_clamp_fusion.2), kind=kCustom, calls=%fused_computation.1 | custom fusion | bytes 6144 | tf_op jit(solution)/shard_map/gather | solution.py:51
  61.0 5.7 %all-to-all-start.4 = ((bf16[128,8,256]{0,2,1:T(8,128)(2,1)}), bf16[128,8,256]{0,2,1:T(8,128)(2,1)}, u32[]{:S(2)}, u32[]{:S(2)}) async-start(bf16[128,8,256]{0,2,1:T(8,128)(2,1)} %bitcast.29), calls=%async_computation.4 | async-start | bytes 1048576 | tf_op jit(solution)/shard_map/all_to_all | solution.py:32
  66.8 2.5 %and_and_fusion.3 = (pred[512,512]{0,1:T(8,128)(4,1)}, pred[512,512]{0,1:T(8,128)(4,1)}, pred[512,512]{0,1:T(8,128)(4,1)S(1)}, pred[512,512]{0,1:T(8,128)(4,1)}, pred[512,512]{0,1:T(8,128)(4,1)}) fusion(s32[512]{0:T(512)S(1)} %get-tuple-element.59, s32[512]{0:T(512)S(1)} %gather_fusion, s32[512]{0:T(512)S(1)} %get-tuple-element.58, s32[512]{0:T(512)S(1)} %gather_fusion.1, ...), kind=kLoop, calls=%fused_computation.90 | loop fusion | flops 5242880 | bytes 1327107 | tf_op jit(solution)/shard_map/and | solution.py:100
  69.2 1.9 %collective-permute-start = (bf16[1024,128]{1,0:T(8,128)(2,1)}, bf16[1024,128]{1,0:T(8,128)(2,1)}, u32[]{:S(2)}, u32[]{:S(2)}) collective-permute-start(bf16[1024,128]{1,0:T(8,128)(2,1)} %bitcast.3), channel_id=1, source_target_pairs={{0,8},{8,16},{16,24},{24,32},{32,40},{40,48},{48,56},{56,64},{64,7... | collective-permute-start | bytes 786440 | tf_op jit(solution)/shard_map/ppermute | solution.py:15
  71.1 7.9 %collective-permute-start.2 = (bf16[1024,128]{1,0:T(8,128)(2,1)}, bf16[1024,128]{1,0:T(8,128)(2,1)}, u32[]{:S(2)}, u32[]{:S(2)}) collective-permute-start(bf16[1024,128]{1,0:T(8,128)(2,1)} %bitcast.3), channel_id=1, source_target_pairs={{8,0},{16,8},{24,16},{32,24},{40,32},{48,40},{56,48},{64,56},{72,6... | collective-permute-start | bytes 786440 | tf_op jit(solution)/shard_map/ppermute | solution.py:15
  79.0 1.9 %collective-permute-start.1 = (bf16[1024,128]{1,0:T(8,128)(2,1)}, bf16[1024,128]{1,0:T(8,128)(2,1)}, u32[]{:S(2)}, u32[]{:S(2)}) collective-permute-start(bf16[1024,128]{1,0:T(8,128)(2,1)} %bitcast.21), channel_id=1, source_target_pairs={{0,8},{8,16},{16,24},{24,32},{32,40},{40,48},{48,56},{56,64},{64,7... | collective-permute-start | bytes 786440 | tf_op jit(solution)/shard_map/ppermute | solution.py:15
  80.9 8.0 %collective-permute-start.3 = (bf16[1024,128]{1,0:T(8,128)(2,1)}, bf16[1024,128]{1,0:T(8,128)(2,1)}, u32[]{:S(2)}, u32[]{:S(2)}) collective-permute-start(bf16[1024,128]{1,0:T(8,128)(2,1)} %bitcast.21), channel_id=1, source_target_pairs={{8,0},{16,8},{24,16},{32,24},{40,32},{48,40},{56,48},{64,56},{72,6... | collective-permute-start | bytes 786440 | tf_op jit(solution)/shard_map/ppermute | solution.py:15
  91.5 2.8 %fusion.123 = (f32[2,512]{1,0:T(2,128)S(1)}, f32[1,2,512,512]{2,3,1,0:T(8,128)}) fusion(bf16[512,2,128]{0,2,1:T(8,128)(2,1)S(1)} %bitcast.336, bf16[1024,128]{1,0:T(8,128)(2,1)} %bitcast.3, s32[]{:T(128)S(6)} %mul.180, pred[512,512]{0,1:T(8,128)(4,1)S(1)} %get-tuple-element.27), kind=kOutput, calls=%fused_computation.197 | convolution fusion | flops 135789568 | bytes 2756612 | tf_op jit(solution)/shard_map/tjgd,ujd->jgtu/dot_general | solution.py:108
  94.3 1.6 fusion.124
  97.0 1.6 copy.189
  98.6 2.4 %mul.193 = f32[1024,2,128]{0,2,1:T(8,128)} reshape(f32[8,128,256]{1,0,2:T(8,128)} %copy.189) | data formatting | bytes 2097152 | tf_op jit(solution)/shard_map/mul | solution.py:21
  101.0 1.3 reduce_sum.56
  102.4 1.5 fusion.120
  103.9 1.6 fusion.122
  107.0 1.7 fusion.18
  108.7 1.7 fusion.17
  110.4 1.6 fusion.121
  113.6 1.9 %collective-permute-start.6 = (bf16[1024,128]{0,1:T(8,128)(2,1)S(1)}, bf16[1024,128]{0,1:T(8,128)(2,1)S(1)}, u32[]{:S(2)}, u32[]{:S(2)}) collective-permute-start(bf16[1024,128]{0,1:T(8,128)(2,1)S(1)} %fusion.21), channel_id=1, source_target_pairs={{8,0},{16,8},{24,16},{32,24},{40,32},{48,40},{56,48},{64,56},{72,6... | collective-permute-start | bytes 786440 | tf_op jit(solution)/shard_map/ppermute | solution.py:15
  116.2 2.4 %collective-permute-start.7 = (bf16[1024,128]{0,1:T(8,128)(2,1)S(1)}, bf16[1024,128]{0,1:T(8,128)(2,1)S(1)}, u32[]{:S(2)}, u32[]{:S(2)}) collective-permute-start(bf16[1024,128]{0,1:T(8,128)(2,1)S(1)} %fusion.20), channel_id=1, source_target_pairs={{0,8},{8,16},{16,24},{24,32},{32,40},{40,48},{48,56},{56,64},{64,7... | collective-permute-start | bytes 786440 | tf_op jit(solution)/shard_map/ppermute | solution.py:15
  118.6 2.7 %fusion.15 = bf16[2,512,512]{1,2,0:T(8,128)(2,1)} fusion(bf16[512,2,128]{0,2,1:T(8,128)(2,1)S(1)} %bitcast.354, f32[1,2,512,512]{2,3,1,0:T(8,128)S(1)} %get-tuple-element.41, f32[2,512]{1,0:T(2,128)S(1)} %get-tuple-element.21, f32[2,512]{1,0:T(2,128)S(1)} %log_add_fusion.1, pred[512,512]{0,1:T(8,128)(4,1)S(1)} %copy-done.9, bf16[1024,128]{1,0:T(8,128)(2,1)} %bitcast.21, ...), kind=kOutput, calls=%fused_computation.39 | convolution fusion | flops 136839168 | bytes 3809284 | tf_op jit(solution)/shard_map/tjgd,ujd->jgtu/dot_general | solution.py:150
  121.3 1.7 fusion.16
  124.9 7.6 %collective-permute-start.4 = (bf16[1024,128]{0,1:T(8,128)(2,1)}, bf16[1024,128]{0,1:T(8,128)(2,1)}, u32[]{:S(2)}, u32[]{:S(2)}) collective-permute-start(bf16[1024,128]{0,1:T(8,128)(2,1)} %fusion.23), channel_id=1, source_target_pairs={{8,0},{16,8},{24,16},{32,24},{40,32},{48,40},{56,48},{64,56},{72,6... | collective-permute-start | bytes 786440 | tf_op jit(solution)/shard_map/ppermute | solution.py:15
  133.7 1.2 fusion.63
  134.9 1.2 convolution_add_fusion.1
  136.8 1.7 fusion.19
  138.5 2.0 %convolution_add_fusion = f32[128,2,512]{2,0,1:T(8,128)} fusion(f32[128,2,512]{2,0,1:T(8,128)S(1)} %convolution_add_fusion.1, bf16[2,512,512]{1,2,0:T(8,128)(2,1)S(1)} %fusion.19, bf16[1024,128]{1,0:T(8,128)(2,1)} %collective-permute-done.2, s32[]{:T(128)S(6)} %select_n.220), kind=kOutput, calls=%fused_computation.44 | convolution fusion | flops 134348800 | bytes 2228228 | tf_op jit(solution)/shard_map/jgtu,ujd->tjgd/dot_general | solution.py:155
  142.4 1.9 %collective-permute-start.5 = (bf16[1024,128]{0,1:T(8,128)(2,1)}, bf16[1024,128]{0,1:T(8,128)(2,1)}, u32[]{:S(2)}, u32[]{:S(2)}) collective-permute-start(bf16[1024,128]{0,1:T(8,128)(2,1)} %fusion.22), channel_id=1, source_target_pairs={{0,8},{8,16},{16,24},{24,32},{32,40},{40,48},{48,56},{56,64},{64,7... | collective-permute-start | bytes 786440 | tf_op jit(solution)/shard_map/ppermute | solution.py:15
  146.4 5.7 %all-to-all-start.7 = ((bf16[8,128,128]{1,2,0:T(8,128)(2,1)}), bf16[8,128,128]{1,2,0:T(8,128)(2,1)}, u32[]{:S(2)}, u32[]{:S(2)}) async-start(bf16[8,128,128]{1,2,0:T(8,128)(2,1)} %copy_bitcast_fusion), calls=%async_computation.7 | async-start | bytes 524288 | tf_op jit(solution)/shard_map/all_to_all | solution.py:202
  152.6 4.6 %collective-permute-done.5 = bf16[1024,128]{0,1:T(8,128)(2,1)} collective-permute-done((bf16[1024,128]{0,1:T(8,128)(2,1)}, bf16[1024,128]{0,1:T(8,128)(2,1)}, u32[]{:S(2)}, u32[]{:S(2)}) %collective-permute-start.5) | collective-permute-done | bytes 262176 | tf_op jit(solution)/shard_map/ppermute | solution.py:15
  157.2 1.5 fusion.57
  159.5 5.5 %all-to-all-start.6 = ((bf16[8,128,128]{1,2,0:T(8,128)(2,1)}), bf16[8,128,128]{1,2,0:T(8,128)(2,1)S(1)}, u32[]{:S(2)}, u32[]{:S(2)}) async-start(bf16[8,128,128]{1,2,0:T(8,128)(2,1)} %copy_bitcast_fusion.1), calls=%async_computation.6 | async-start | bytes 524288 | tf_op jit(solution)/shard_map/all_to_all | solution.py:201
  165.0 1.2 fusion.73
  166.3 1.2 broadcast_select_fusion.1
  168.6 3.7 %all-to-all-done.6 = bf16[8,128,128]{1,2,0:T(8,128)(2,1)S(1)} async-done(((bf16[8,128,128]{1,2,0:T(8,128)(2,1)}), bf16[8,128,128]{1,2,0:T(8,128)(2,1)S(1)}, u32[]{:S(2)}, u32[]{:S(2)}) %all-to-all-start.6) | async-done | bytes 262176 | tf_op jit(solution)/shard_map/all_to_all | solution.py:201
  172.3 3.5 %all-to-all-start.5 = ((bf16[8,128,256]{2,1,0:T(8,128)(2,1)}), bf16[8,128,256]{2,1,0:T(8,128)(2,1)S(1)}, u32[]{:S(2)}, u32[]{:S(2)}) async-start(bf16[8,128,256]{2,1,0:T(8,128)(2,1)} %bitcast.74), calls=%async_computation.5 | async-start | bytes 1048576 | tf_op jit(solution)/shard_map/all_to_all | solution.py:200
  175.8 1.8 copy.225
  178.5 6.0 %all-to-all-done.5 = bf16[8,128,256]{2,1,0:T(8,128)(2,1)S(1)} async-done(((bf16[8,128,256]{2,1,0:T(8,128)(2,1)}), bf16[8,128,256]{2,1,0:T(8,128)(2,1)S(1)}, u32[]{:S(2)}, u32[]{:S(2)}) %all-to-all-start.5) | async-done | bytes 524320 | tf_op jit(solution)/shard_map/all_to_all | solution.py:200
  (110 shorter events, 26.1 us)
Async XLA Ops:
  0.6 1.0 copy-start
  0.6 18.3 %copy-start.19 = (bf16[128,2048]{1,0:T(8,128)(2,1)S(1)}, bf16[128,2048]{1,0:T(8,128)(2,1)}, u32[]{:S(2)}) copy-start(bf16[128,2048]{1,0:T(8,128)(2,1)} %param.11) | copy-start | bytes 1572868
  0.7 29.1 %copy-start.22 = (s32[128]{0:T(128)S(1)}, s32[128]{0:T(128)}, u32[]{:S(2)}) copy-start(s32[128]{0:T(128)} %param.13) | copy-start | bytes 1540
  0.7 35.6 %copy-start.20 = (bf16[128,2048]{1,0:T(8,128)(2,1)S(1)}, bf16[128,2048]{1,0:T(8,128)(2,1)}, u32[]{:S(2)}) copy-start(bf16[128,2048]{1,0:T(8,128)(2,1)} %param.7) | copy-start | bytes 1572868
  2.3 12.6 %all-to-all-start = ((bf16[128,8,128]{2,0,1:T(8,128)(2,1)}), bf16[128,8,128]{2,0,1:T(8,128)(2,1)}, u32[]{:S(2)}, u32[]{:S(2)}) async-start(bf16[128,8,128]{2,0,1:T(8,128)(2,1)} %copy_bitcast_fusion.3), calls=%async_computation | async-start | bytes 524288 | tf_op jit(solution)/shard_map/all_to_all | solution.py:30
  14.9 11.3 %all-to-all-start.2 = ((bf16[128,8,128]{2,0,1:T(8,128)(2,1)}), bf16[128,8,128]{2,0,1:T(8,128)(2,1)}, u32[]{:S(2)}, u32[]{:S(2)}) async-start(bf16[128,8,128]{2,0,1:T(8,128)(2,1)} %copy_bitcast_fusion.2), calls=%async_computation.2 | async-start | bytes 524288 | tf_op jit(solution)/shard_map/all_to_all | solution.py:31
  19.0 23.9 %copy-start.1 = (s32[65536]{0:T(1024)S(1)}, s32[65536]{0:T(1024)}, u32[]{:S(2)}) copy-start(s32[65536]{0:T(1024)} %param.12) | copy-start | bytes 786436
  26.3 12.1 %all-to-all-start.3 = ((bf16[128,8,256]{0,2,1:T(8,128)(2,1)}), bf16[128,8,256]{0,2,1:T(8,128)(2,1)S(1)}, u32[]{:S(2)}, u32[]{:S(2)}) async-start(bf16[128,8,256]{0,2,1:T(8,128)(2,1)} %bitcast.23), calls=%async_computation.3 | async-start | bytes 1048576 | tf_op jit(solution)/shard_map/all_to_all | solution.py:33
  38.4 22.6 %all-to-all-start.1 = ((bf16[128,8,256]{0,2,1:T(8,128)(2,1)}), bf16[128,8,256]{0,2,1:T(8,128)(2,1)S(1)}, u32[]{:S(2)}, u32[]{:S(2)}) async-start(bf16[128,8,256]{0,2,1:T(8,128)(2,1)} %bitcast.7), calls=%async_computation.1 | async-start | bytes 1048576 | tf_op jit(solution)/shard_map/all_to_all | solution.py:29
  53.7 6.3 %copy-start.21 = (bf16[128,2048]{1,0:T(8,128)(2,1)S(1)}, bf16[128,2048]{1,0:T(8,128)(2,1)}, u32[]{:S(2)}) copy-start(bf16[128,2048]{1,0:T(8,128)(2,1)} %param.10) | copy-start | bytes 1572868
  61.0 34.8 %all-to-all-start.4 = ((bf16[128,8,256]{0,2,1:T(8,128)(2,1)}), bf16[128,8,256]{0,2,1:T(8,128)(2,1)}, u32[]{:S(2)}, u32[]{:S(2)}) async-start(bf16[128,8,256]{0,2,1:T(8,128)(2,1)} %bitcast.29), calls=%async_computation.4 | async-start | bytes 1048576 | tf_op jit(solution)/shard_map/all_to_all | solution.py:32
  69.2 22.3 %copy-start.13 = (pred[512,512]{0,1:T(8,128)(4,1)}, pred[512,512]{0,1:T(8,128)(4,1)S(1)}, u32[]{:S(2)}) copy-start(pred[512,512]{0,1:T(8,128)(4,1)S(1)} %get-tuple-element.27) | copy-start | bytes 786436
  69.2 41.1 %collective-permute-start = (bf16[1024,128]{1,0:T(8,128)(2,1)}, bf16[1024,128]{1,0:T(8,128)(2,1)}, u32[]{:S(2)}, u32[]{:S(2)}) collective-permute-start(bf16[1024,128]{1,0:T(8,128)(2,1)} %bitcast.3), channel_id=1, source_target_pairs={{0,8},{8,16},{16,24},{24,32},{32,40},{40,48},{48,56},{56,64},{64,7... | collective-permute-start | bytes 786440 | tf_op jit(solution)/shard_map/ppermute | solution.py:15
  71.1 32.7 %collective-permute-start.2 = (bf16[1024,128]{1,0:T(8,128)(2,1)}, bf16[1024,128]{1,0:T(8,128)(2,1)}, u32[]{:S(2)}, u32[]{:S(2)}) collective-permute-start(bf16[1024,128]{1,0:T(8,128)(2,1)} %bitcast.3), channel_id=1, source_target_pairs={{8,0},{16,8},{24,16},{32,24},{40,32},{48,40},{56,48},{64,56},{72,6... | collective-permute-start | bytes 786440 | tf_op jit(solution)/shard_map/ppermute | solution.py:15
  79.0 42.3 %collective-permute-start.1 = (bf16[1024,128]{1,0:T(8,128)(2,1)}, bf16[1024,128]{1,0:T(8,128)(2,1)}, u32[]{:S(2)}, u32[]{:S(2)}) collective-permute-start(bf16[1024,128]{1,0:T(8,128)(2,1)} %bitcast.21), channel_id=1, source_target_pairs={{0,8},{8,16},{16,24},{24,32},{32,40},{40,48},{48,56},{56,64},{64,7... | collective-permute-start | bytes 786440 | tf_op jit(solution)/shard_map/ppermute | solution.py:15
  80.9 55.9 %collective-permute-start.3 = (bf16[1024,128]{1,0:T(8,128)(2,1)}, bf16[1024,128]{1,0:T(8,128)(2,1)}, u32[]{:S(2)}, u32[]{:S(2)}) collective-permute-start(bf16[1024,128]{1,0:T(8,128)(2,1)} %bitcast.21), channel_id=1, source_target_pairs={{8,0},{16,8},{24,16},{32,24},{40,32},{48,40},{56,48},{64,56},{72,6... | collective-permute-start | bytes 786440 | tf_op jit(solution)/shard_map/ppermute | solution.py:15
  98.6 3.8 %copy-start.9 = (pred[512,512]{0,1:T(8,128)(4,1)S(1)}, pred[512,512]{0,1:T(8,128)(4,1)}, u32[]{:S(2)}) copy-start(pred[512,512]{0,1:T(8,128)(4,1)} %get-tuple-element.26) | copy-start | bytes 786436
  101.0 2.9 %copy-start.11 = (pred[512,512]{0,1:T(8,128)(4,1)S(1)}, pred[512,512]{0,1:T(8,128)(4,1)}, u32[]{:S(2)}) copy-start(pred[512,512]{0,1:T(8,128)(4,1)} %get-tuple-element.28) | copy-start | bytes 786436
  102.4 3.2 %copy-start.10 = (pred[512,512]{0,1:T(8,128)(4,1)S(1)}, pred[512,512]{0,1:T(8,128)(4,1)}, u32[]{:S(2)}) copy-start(pred[512,512]{0,1:T(8,128)(4,1)} %get-tuple-element.29) | copy-start | bytes 786436
  103.9 2.1 %copy-start.2 = (f32[1,2,512,512]{2,3,1,0:T(8,128)S(1)}, f32[1,2,512,512]{2,3,1,0:T(8,128)}, u32[]{:S(2)}) copy-start(f32[1,2,512,512]{2,3,1,0:T(8,128)} %get-tuple-element.47) | copy-start | bytes 6291460
  103.9 2.1 %copy-start.14 = (pred[512,512]{0,1:T(8,128)(4,1)S(1)}, pred[512,512]{0,1:T(8,128)(4,1)}, u32[]{:S(2)}) copy-start(pred[512,512]{0,1:T(8,128)(4,1)} %copy-done.13) | copy-start | bytes 786436
  105.5 1.0 copy-start.12
  106.0 1.0 copy-start.8
  108.7 1.7 copy-start.15
  110.3 23.3 %copy-start.3 = (bf16[2,512,512]{1,2,0:T(8,128)(2,1)}, bf16[2,512,512]{1,2,0:T(8,128)(2,1)S(1)}, u32[]{:S(2)}) copy-start(bf16[2,512,512]{1,2,0:T(8,128)(2,1)S(1)} %fusion.17) | copy-start | bytes 3145732
  112.0 1.0 copy-start.16
  113.6 31.4 %collective-permute-start.6 = (bf16[1024,128]{0,1:T(8,128)(2,1)S(1)}, bf16[1024,128]{0,1:T(8,128)(2,1)S(1)}, u32[]{:S(2)}, u32[]{:S(2)}) collective-permute-start(bf16[1024,128]{0,1:T(8,128)(2,1)S(1)} %fusion.21), channel_id=1, source_target_pairs={{8,0},{16,8},{24,16},{32,24},{40,32},{48,40},{56,48},{64,56},{72,6... | collective-permute-start | bytes 786440 | tf_op jit(solution)/shard_map/ppermute | solution.py:15
  116.2 28.8 %collective-permute-start.7 = (bf16[1024,128]{0,1:T(8,128)(2,1)S(1)}, bf16[1024,128]{0,1:T(8,128)(2,1)S(1)}, u32[]{:S(2)}, u32[]{:S(2)}) collective-permute-start(bf16[1024,128]{0,1:T(8,128)(2,1)S(1)} %fusion.20), channel_id=1, source_target_pairs={{0,8},{8,16},{16,24},{24,32},{32,40},{40,48},{48,56},{56,64},{64,7... | collective-permute-start | bytes 786440 | tf_op jit(solution)/shard_map/ppermute | solution.py:15
  123.0 11.9 %copy-start.5 = (bf16[2,512,512]{1,2,0:T(8,128)(2,1)}, bf16[2,512,512]{1,2,0:T(8,128)(2,1)S(1)}, u32[]{:S(2)}) copy-start(bf16[2,512,512]{1,2,0:T(8,128)(2,1)S(1)} %fusion.16) | copy-start | bytes 3145732
  124.9 27.7 %collective-permute-start.4 = (bf16[1024,128]{0,1:T(8,128)(2,1)}, bf16[1024,128]{0,1:T(8,128)(2,1)}, u32[]{:S(2)}, u32[]{:S(2)}) collective-permute-start(bf16[1024,128]{0,1:T(8,128)(2,1)} %fusion.23), channel_id=1, source_target_pairs={{8,0},{16,8},{24,16},{32,24},{40,32},{48,40},{56,48},{64,56},{72,6... | collective-permute-start | bytes 786440 | tf_op jit(solution)/shard_map/ppermute | solution.py:15
  142.4 14.8 %collective-permute-start.5 = (bf16[1024,128]{0,1:T(8,128)(2,1)}, bf16[1024,128]{0,1:T(8,128)(2,1)}, u32[]{:S(2)}, u32[]{:S(2)}) collective-permute-start(bf16[1024,128]{0,1:T(8,128)(2,1)} %fusion.22), channel_id=1, source_target_pairs={{0,8},{8,16},{16,24},{24,32},{32,40},{40,48},{48,56},{56,64},{64,7... | collective-permute-start | bytes 786440 | tf_op jit(solution)/shard_map/ppermute | solution.py:15
  144.9 7.1 %copy-start.4 = (bf16[2,512,512]{1,2,0:T(8,128)(2,1)S(1)}, bf16[2,512,512]{1,2,0:T(8,128)(2,1)}, u32[]{:S(2)}) copy-start(bf16[2,512,512]{1,2,0:T(8,128)(2,1)} %copy-done.3) | copy-start | bytes 3145732
  145.6 11.6 %copy-start.7 = (bf16[2,512,512]{1,2,0:T(8,128)(2,1)S(1)}, bf16[2,512,512]{1,2,0:T(8,128)(2,1)}, u32[]{:S(2)}) copy-start(bf16[2,512,512]{1,2,0:T(8,128)(2,1)} %fusion.15) | copy-start | bytes 3145732
  145.7 11.6 %copy-start.18 = (f32[128,512]{1,0:T(8,128)S(1)}, f32[128,512]{1,0:T(8,128)}, u32[]{:S(2)}) copy-start(f32[128,512]{1,0:T(8,128)} %convolution_bitcast_fusion.8) | copy-start | bytes 786436
  146.4 13.1 %all-to-all-start.7 = ((bf16[8,128,128]{1,2,0:T(8,128)(2,1)}), bf16[8,128,128]{1,2,0:T(8,128)(2,1)}, u32[]{:S(2)}, u32[]{:S(2)}) async-start(bf16[8,128,128]{1,2,0:T(8,128)(2,1)} %copy_bitcast_fusion), calls=%async_computation.7 | async-start | bytes 524288 | tf_op jit(solution)/shard_map/all_to_all | solution.py:202
  158.7 7.6 %copy-start.6 = (bf16[2,512,512]{1,2,0:T(8,128)(2,1)S(1)}, bf16[2,512,512]{1,2,0:T(8,128)(2,1)}, u32[]{:S(2)}) copy-start(bf16[2,512,512]{1,2,0:T(8,128)(2,1)} %copy-done.5) | copy-start | bytes 3145732
  158.7 7.6 %copy-start.17 = (f32[128,2,512]{2,0,1:T(8,128)S(1)}, f32[128,2,512]{2,0,1:T(8,128)}, u32[]{:S(2)}) copy-start(f32[128,2,512]{2,0,1:T(8,128)} %convolution_add_fusion) | copy-start | bytes 1572868
  159.5 12.9 %all-to-all-start.6 = ((bf16[8,128,128]{1,2,0:T(8,128)(2,1)}), bf16[8,128,128]{1,2,0:T(8,128)(2,1)S(1)}, u32[]{:S(2)}, u32[]{:S(2)}) async-start(bf16[8,128,128]{1,2,0:T(8,128)(2,1)} %copy_bitcast_fusion.1), calls=%async_computation.6 | async-start | bytes 524288 | tf_op jit(solution)/shard_map/all_to_all | solution.py:201
  172.3 12.1 %all-to-all-start.5 = ((bf16[8,128,256]{2,1,0:T(8,128)(2,1)}), bf16[8,128,256]{2,1,0:T(8,128)(2,1)S(1)}, u32[]{:S(2)}, u32[]{:S(2)}) async-start(bf16[8,128,256]{2,1,0:T(8,128)(2,1)} %bitcast.74), calls=%async_computation.5 | async-start | bytes 1048576 | tf_op jit(solution)/shard_map/all_to_all | solution.py:200
where the time goes:
time: 187 us; the launch traced here: 186 us
  starting transfers between devices  71.1 us (38%)
  local copies, waits for them, and re-layouts  34 us (18%)
  matrix products  33.9 us (18%)
  waiting for transfers between devices  27.5 us (15%)
  between operations  10.4 us (6%)
  other arithmetic  8.82 us (5%)
    ppermute x8, starting transfers between devices, shifted(): lax.ppermute(value, axis, [(source, source + steps) for source in range(i...  33.5 us
    gather x4, local copies, waits for them, and re-layouts, half_of(): return (slot, positions, segment_ids[positions])  12.6 us
    dot_general x5, matrix products, local(): jnp.einsum('tjgd,ujd->jgtu', grad_four, value_three, preferred_element_ty...  9.36 us
    dot_general x5, matrix products, scores_of(): jnp.einsum('tjgd,ujd->jgtu', query_four, key_three, preferred_element_typ...  9 us
    unnamed x52, local copies, waits for them, and re-layouts  7.74 us
    dot_general x5, matrix products, local(): jnp.einsum('jgtu,ujd->tjgd', score_grads_b, tile_key_three, preferred_ele...  6.96 us
    all_to_all x1, waiting for transfers between devices, local(): lax.all_to_all(values, 'head', split_axis=1, concat_axis=0, tiled=True)  6.27 us
    all_to_all x1, waiting for transfers between devices, local(): lax.all_to_all(query_block_grads, 'head', split_axis=0, concat_axis=1, ti...  5.98 us
  transfers between devices with their start and end apart: 16, of which 6 were waited for; matrix products, arithmetic and copies ran while one was open for 40% of the time, Pallas kernels for 0%

commit v1 on v0

v1 whole, which is shorter than its diff:
```python
import functools

import jax
import jax.numpy as jnp
from jax import lax
from jax.experimental import pallas as pl
from jax.experimental.pallas import tpu as pltpu
from jax.sharding import PartitionSpec as P

HEAD = 128
CHUNK = 128
HALF = 512
WINDOW = HALF + CHUNK
GROUPS = 8
SCALE = HEAD ** -0.5
LOG2E = 1.4426950408889634
HIDDEN = -1e30
MESH = pl.DeviceIdType.MESH
BF16 = jnp.bfloat16
F32 = jnp.float32
NT = (((1,), (1,)), ((), ()))
KINDS = 5


def kernel(
    q_hbm, k_hbm, v_hbm, o_hbm, g_hbm, seg, order,
    dq_out, dk_out, dv_out,
    q_all, g_all, k_all, v_all, kt_all, d_all, d_mine, o_rows, g_rows,
    halo, back, dk_sum, dv_sum, dq_stage, dk_stage, dv_stage, bias,
    load_sem, own_sem, in_send, in_recv, halo_send, halo_recv, back_send, back_recv,
    out_send, out_recv, out_own,
):
    i = lax.axis_index("blk")
    h = lax.axis_index("head")
    blocks = lax.axis_size("blk")
    x, z = h // 2, h % 2
    above = lax.rem(i + 1, blocks)
    below = lax.rem(i + blocks - 1, blocks)
    partners = [
        lax.rem(x + dx, 4) * 2 + lax.rem(z + dz, 2)
        for dx in (2, 1, 3, 0)
        for dz in (1, 0)
        if dx or dz
    ]

    barrier = pltpu.get_barrier_semaphore()
    for o in partners:
        pl.semaphore_signal(barrier, inc=1, device_id=(i, o), device_id_type=MESH)
    for b in (above, below):
        pl.semaphore_signal(barrier, inc=1, device_id=(b, h), device_id_type=MESH)

    loads = [
        pltpu.make_async_copy(o_hbm, o_rows, load_sem.at[0]),
        pltpu.make_async_copy(g_hbm, g_rows, load_sem.at[1]),
    ]
    for c in loads:
        c.start()

    def own_rows(o):
        return o // 4, pl.multiple_of(HALF + lax.rem(o, 4) * CHUNK, CHUNK)

    def cols(o, width):
        return pl.ds(pl.multiple_of(o * width, width), width)

    def piece(kind, target, source):
        s, row = own_rows(source)
        if kind == 0:
            return k_hbm.at[:, cols(target, HEAD)], k_all.at[s, pl.ds(row, CHUNK), :]
        if kind == 1:
            return v_hbm.at[:, cols(target, HEAD)], v_all.at[s, pl.ds(row, CHUNK), :]
        if kind == 2:
            return d_mine.at[target], d_all.at[source]
        if kind == 3:
            return q_hbm.at[:, cols(target, 2 * HEAD)], q_all.at[source]
        return g_hbm.at[:, cols(target, 2 * HEAD)], g_all.at[source]

    def send(kind, o):
        src, dst = piece(kind, o, h)
        return pltpu.make_async_remote_copy(
            src, dst, in_send.at[kind, o], in_recv.at[kind, h],
            device_id=(i, o), device_id_type=MESH,
        )

    def arrival(kind, o):
        src, dst = piece(kind, h, o)
        return pltpu.make_async_remote_copy(
            src, dst, in_send.at[kind, o], in_recv.at[kind, o],
            device_id=(i, o), device_id_type=MESH,
        )

    def own(kind):
        src, dst = piece(kind, h, h)
        return pltpu.make_async_copy(src, dst, own_sem.at[kind])

    for c in loads:
        c.wait()
    d_mine[...] = jnp.zeros_like(d_mine)
    for head in range(2 * GROUPS):
        at = slice(head * HEAD, (head + 1) * HEAD)
        product = o_rows[:, at].astype(F32) * g_rows[:, at].astype(F32)
        d_mine[head // 2, head % 2 : head % 2 + 1, :] = jnp.sum(
            product.T, axis=0, keepdims=True
        )

    pl.semaphore_wait(barrier, GROUPS + 1)
    for kind in range(KINDS):
        for o in partners:
            send(kind, o).start()
        own(kind).start()

    slot_half = [order[2 * i], order[2 * i + 1]]
    early = (slot_half[0] > slot_half[1]).astype(jnp.int32)
    is_early = [early == 0, early == 1]
    key_at = lax.broadcasted_iota(jnp.int32, (CHUNK, CHUNK), 0)
    row_at = lax.broadcasted_iota(jnp.int32, (CHUNK, CHUNK), 1)
    causal = key_at <= row_at
    for s in range(2):
        first = slot_half[s] * 4
        documents = []
        for c in range(8):
            line = seg[pl.ds(jnp.maximum(first - 4 + c, 0), 1), :].astype(F32)
            if c < 4:
                line = jnp.where(first == 0, -1.0, line)
            documents.append(line)
        for c in range(8):
            column = jnp.broadcast_to(documents[c], (CHUNK, CHUNK)).T
            for p in range(4):
                r = c - p
                if 0 <= r <= 4:
                    visible = column == documents[4 + p]
                    if r == 4:
                        visible = visible & causal
                    bias[s, p, r * CHUNK : (r + 1) * CHUNK, :] = jnp.where(
                        visible, 0.0, HIDDEN
                    )
    dk_sum[...] = jnp.zeros_like(dk_sum)
    dv_sum[...] = jnp.zeros_like(dv_sum)

    for kind in (0, 1):
        for o in partners:
            arrival(kind, o).wait_recv()
        own(kind).wait()
    late = 1 - early
    for n, slot in ((2, early), (3, late)):
        halo[n, 0] = k_all[slot, HALF:, :]
        halo[n, 1] = v_all[slot, HALF:, :]
    halo_up = pltpu.make_async_remote_copy(
        halo.at[2], halo.at[0], halo_send.at[0], halo_recv.at[0],
        device_id=(above, h), device_id_type=MESH,
    )
    halo_down = pltpu.make_async_remote_copy(
        halo.at[3], halo.at[1], halo_send.at[1], halo_recv.at[1],
        device_id=(below, h), device_id_type=MESH,
    )
    halo_up.start()
    halo_down.start()
    for s in range(2):
        kt_all[s, :, HALF:] = k_all[s, HALF:, :].T
    halo_up.wait_recv()
    halo_down.wait_recv()
    for s in range(2):
        at = jnp.where(is_early[s], 0, jnp.where(i == blocks - 1, 2, 1))
        before = halo[at, 0]
        k_all[s, :HALF, :] = before
        kt_all[s, :, :HALF] = before.T
        v_all[s, :HALF, :] = halo[at, 1]

    for kind in (2, 3, 4):
        for o in partners:
            arrival(kind, o).wait_recv()
        own(kind).wait()

    def out_piece(kind, target, source):
        if kind == 0:
            return dq_stage.at[target], dq_out.at[:, cols(source, 2 * HEAD)]
        if kind == 1:
            return dk_stage.at[target], dk_out.at[:, cols(source, HEAD)]
        return dv_stage.at[target], dv_out.at[:, cols(source, HEAD)]

    def out_remote(kind, target, source, o):
        src, dst = out_piece(kind, target, source)
        return pltpu.make_async_remote_copy(
            src, dst, out_send.at[kind, target], out_recv.at[kind, source],
            device_id=(i, o), device_id_type=MESH,
        )

    def out_local(kind):
        src, dst = out_piece(kind, h, h)
        return pltpu.make_async_copy(src, dst, out_own.at[kind])

    def give(kind, o):
        @pl.when(o != h)
        def _():
            out_remote(kind, o, h, o).start()

        @pl.when(o == h)
        def _():
            out_local(kind).start()

    def tile(s, p):
        o = s * 4 + p
        keys_at = pl.ds(pl.multiple_of(p * CHUNK, CHUNK), WINDOW)
        keys = k_all[s, keys_at, :]
        vals = v_all[s, keys_at, :]
        q_two = jnp.concatenate([q_all[o, :, :HEAD], q_all[o, :, HEAD:]], axis=0)
        g_two = jnp.concatenate([g_all[o, :, :HEAD], g_all[o, :, HEAD:]], axis=0)
        delta = jnp.concatenate([d_all[o, 0:1, :], d_all[o, 1:2, :]], axis=1)
        hide = bias[s, p]
        scores = lax.dot_general(keys, q_two, NT, preferred_element_type=F32)
        scores = scores * (SCALE * LOG2E) + jnp.concatenate([hide, hide], axis=1)
        top = jnp.max(scores, axis=0, keepdims=True)
        terms = jnp.exp2(scores - top)
        weights = terms * (1.0 / jnp.sum(terms, axis=0, keepdims=True))
        weights_b = weights.astype(BF16)
        pulls = lax.dot_general(vals, g_two, NT, preferred_element_type=F32)
        score_grads = (weights * (pulls - delta)).astype(BF16)
        dv_sum[s, keys_at, :] += jnp.dot(weights_b, g_two, preferred_element_type=F32)
        dk_sum[s, keys_at, :] += jnp.dot(score_grads, q_two, preferred_element_type=F32)
        dq = jnp.dot(kt_all[s, :, keys_at], score_grads, preferred_element_type=F32) * SCALE
        dq_stage[o, :, :HEAD] = dq[:, :HEAD].T.astype(BF16)
        dq_stage[o, :, HEAD:] = dq[:, HEAD:].T.astype(BF16)

    def step(d, carry):
        p = lax.rem(h + 1 + d, 4)
        for s in range(2):
            tile(s, p)
        for s in range(2):
            give(0, s * 4 + p)
        return carry

    lax.fori_loop(0, 4, step, 0)

    for n, slot in ((2, early), (3, late)):
        back[n, 0] = dk_sum[slot, :HALF, :].astype(BF16)
        back[n, 1] = dv_sum[slot, :HALF, :].astype(BF16)
    back_down = pltpu.make_async_remote_copy(
        back.at[2], back.at[1], back_send.at[0], back_recv.at[0],
        device_id=(below, h), device_id_type=MESH,
    )
    back_up = pltpu.make_async_remote_copy(
        back.at[3], back.at[0], back_send.at[1], back_recv.at[1],
        device_id=(above, h), device_id_type=MESH,
    )
    back_down.start()
    back_up.start()
    back_down.wait_recv()
    back_up.wait_recv()
    for s in range(2):
        at = jnp.where(is_early[s], jnp.where(i == blocks - 1, 3, 1), 0)
        nothing = jnp.logical_and(jnp.logical_not(is_early[s]), i == 0)
        for p in range(4):
            own_at = slice(HALF + p * CHUNK, HALF + (p + 1) * CHUNK)
            rows = slice(p * CHUNK, (p + 1) * CHUNK)
            dk_more = jnp.where(nothing, 0.0, back[at, 0, rows, :].astype(F32))
            dv_more = jnp.where(nothing, 0.0, back[at, 1, rows, :].astype(F32))
            dk_stage[s * 4 + p] = ((dk_sum[s, own_at, :] + dk_more) * SCALE).astype(BF16)
            dv_stage[s * 4 + p] = (dv_sum[s, own_at, :] + dv_more).astype(BF16)
    for kind in (1, 2):
        for o in partners:
            out_remote(kind, o, h, o).start()
        out_local(kind).start()

    halo_up.wait_send()
    halo_down.wait_send()
    back_down.wait_send()
    back_up.wait_send()
    for kind in range(KINDS):
        for o in partners:
            send(kind, o).wait_send()
    for kind in range(3):
        for o in partners:
            out_remote(kind, o, h, o).wait_send()
            out_remote(kind, h, o, o).wait_recv()
        out_local(kind).wait()


def local(queries, keys, values, outputs, out_grads, segment_ids, block_order):
    rows = queries.shape[0]
    hbm = pl.BlockSpec(memory_space=pl.ANY)
    vmem = pl.BlockSpec(memory_space=pltpu.VMEM)
    smem = pl.BlockSpec(memory_space=pltpu.SMEM)
    dma = pltpu.SemaphoreType.DMA
    return pl.pallas_call(
        kernel,
        out_shape=[
            jax.ShapeDtypeStruct((rows, queries.shape[1]), BF16),
            jax.ShapeDtypeStruct((rows, keys.shape[1]), BF16),
            jax.ShapeDtypeStruct((rows, values.shape[1]), BF16),
        ],
        in_specs=[hbm] * 5 + [vmem, smem],
        out_specs=[hbm] * 3,
        scratch_shapes=[
            pltpu.VMEM((GROUPS, CHUNK, 2 * HEAD), BF16),
            pltpu.VMEM((GROUPS, CHUNK, 2 * HEAD), BF16),
            pltpu.VMEM((2, 2 * HALF, HEAD), BF16),
            pltpu.VMEM((2, 2 * HALF, HEAD), BF16),
            pltpu.VMEM((2, HEAD, 2 * HALF), BF16),
            pltpu.VMEM((GROUPS, 8, CHUNK), F32),
            pltpu.VMEM((GROUPS, 8, CHUNK), F32),
            pltpu.VMEM((CHUNK, 2 * GROUPS * HEAD), BF16),
            pltpu.VMEM((CHUNK, 2 * GROUPS * HEAD), BF16),
            pltpu.VMEM((4, 2, HALF, HEAD), BF16),
            pltpu.VMEM((4, 2, HALF, HEAD), BF16),
            pltpu.VMEM((2, 2 * HALF, HEAD), F32),
            pltpu.VMEM((2, 2 * HALF, HEAD), F32),
            pltpu.VMEM((GROUPS, CHUNK, 2 * HEAD), BF16),
            pltpu.VMEM((GROUPS, CHUNK, HEAD), BF16),
            pltpu.VMEM((GROUPS, CHUNK, HEAD), BF16),
            pltpu.VMEM((2, 4, WINDOW, CHUNK), F32),
            dma((2,)),
            dma((KINDS,)),
            dma((KINDS, GROUPS)),
            dma((KINDS, GROUPS)),
            dma((2,)),
            dma((2,)),
            dma((2,)),
            dma((2,)),
            dma((3, GROUPS)),
            dma((3, GROUPS)),
            dma((3,)),
        ],
        compiler_params=pltpu.CompilerParams(
            collective_id=0, has_side_effects=True, vmem_limit_bytes=40 * 1024 * 1024
        ),
        name="attention_backward",
    )(
        queries, keys, values, outputs, out_grads,
        segment_ids.reshape(-1, CHUNK), block_order,
    )


def solution(mesh):
    row = P(("blk", "head"), None)
    return jax.shard_map(
        local,
        mesh=mesh,
        in_specs=(row,) * 5 + (P(), P()),
        out_specs=(row,) * 3,
        check_vma=False,
    )
```

time: 187 us -> 66.1 us (0.35)
  the two profiles are of different devices: /device:TPU:256 before, /device:TPU:64 now
where the time goes in v1:
time: 66.1 us; the launch traced here: 65.7 us
  Pallas kernels  56.3 us (85%)
  local copies, waits for them, and re-layouts  8.82 us (13%)
    pallas_call x1, Pallas kernels, local(): pl.pallas_call(kernel, out_shape=[jax.ShapeDtypeStruct((rows, queries.sha...  56.3 us
    unnamed x17, local copies, waits for them, and re-layouts  8.82 us

profile of v1, /device:TPU:64, one launch (start us, length us, event | category | flops | bytes accessed | tf_op | source)
XLA Modules:
  0.0 65.7 jit_solution(187308180057271169)
XLA Ops:
  0.6 0.0 copy-start.6
  0.6 0.6 copy-done.6
  1.3 0.0 copy-start
  1.3 1.0 %copy-done = bf16[128,2048]{1,0:T(8,128)(2,1)S(1)} copy-done((bf16[128,2048]{1,0:T(8,128)(2,1)S(1)}, bf16[128,2048]{1,0:T(8,128)(2,1)}, u32[]{:S(2)}) %copy-start) | copy-done | bytes 524312
  2.3 0.0 copy-start.1
  2.3 1.0 %copy-done.1 = bf16[128,2048]{1,0:T(8,128)(2,1)S(1)} copy-done((bf16[128,2048]{1,0:T(8,128)(2,1)S(1)}, bf16[128,2048]{1,0:T(8,128)(2,1)}, u32[]{:S(2)}) %copy-start.1) | copy-done | bytes 524312
  3.4 0.0 copy-start.2
  3.4 1.0 %copy-done.2 = bf16[128,2048]{1,0:T(8,128)(2,1)S(1)} copy-done((bf16[128,2048]{1,0:T(8,128)(2,1)S(1)}, bf16[128,2048]{1,0:T(8,128)(2,1)}, u32[]{:S(2)}) %copy-start.2) | copy-done | bytes 524312
  4.4 0.0 copy-start.3
  4.4 0.9 %copy-done.3 = bf16[128,1024]{1,0:T(8,128)(2,1)S(1)} copy-done((bf16[128,1024]{1,0:T(8,128)(2,1)S(1)}, bf16[128,1024]{1,0:T(8,128)(2,1)}, u32[]{:S(2)}) %copy-start.3) | copy-done | bytes 262168
  5.4 0.0 copy-start.4
  5.4 0.9 %copy-done.4 = bf16[128,1024]{1,0:T(8,128)(2,1)S(1)} copy-done((bf16[128,1024]{1,0:T(8,128)(2,1)S(1)}, bf16[128,1024]{1,0:T(8,128)(2,1)}, u32[]{:S(2)}) %copy-start.4) | copy-done | bytes 262168
  6.3 0.0 copy-start.5
  6.3 0.9 %copy-done.5 = s32[65536]{0:T(1024)S(1)} copy-done((s32[65536]{0:T(1024)S(1)}, s32[65536]{0:T(1024)}, u32[]{:S(2)}) %copy-start.5) | copy-done | bytes 262168
  7.3 56.3 %attention_backward.1 = (bf16[128,2048]{1,0:T(8,128)(2,1)S(1)}, bf16[128,1024]{1,0:T(8,128)(2,1)S(1)}, bf16[128,1024]{1,0:T(8,128)(2,1)S(1)}) custom-call(bf16[128,2048]{1,0:T(8,128)(2,1)S(1)} %copy-done, bf16[128,1024]{1,0:T(8,128)(2,1)S(1)} %copy-done.3, bf16[128,1024]{1,0:T(8,128)(2,1)S(1)} %copy-done.4, bf16[128,2048]{1,0:T(8,128)(2,1)S(1)} %copy-done.1, ...), custom_call_target="tpu_custom_call" | custom-call | tf_op jit(solution)/shard_map/attention_backward/pallas_call | solution.py:283
  63.5 0.8 %copy.13 = bf16[128,2048]{1,0:T(8,128)(2,1)} copy(bf16[128,2048]{1,0:T(8,128)(2,1)S(1)} %get-tuple-element.6) | data formatting | bytes 1048576
  64.3 0.7 %copy.14 = bf16[128,1024]{1,0:T(8,128)(2,1)} copy(bf16[128,1024]{1,0:T(8,128)(2,1)S(1)} %get-tuple-element.7) | data formatting | bytes 524288
  65.0 0.7 %copy.15 = bf16[128,1024]{1,0:T(8,128)(2,1)} copy(bf16[128,1024]{1,0:T(8,128)(2,1)S(1)} %get-tuple-element.8) | data formatting | bytes 524288
Async XLA Ops:
  0.6 0.7 copy-start.6
  1.3 1.0 %copy-start = (bf16[128,2048]{1,0:T(8,128)(2,1)S(1)}, bf16[128,2048]{1,0:T(8,128)(2,1)}, u32[]{:S(2)}) copy-start(bf16[128,2048]{1,0:T(8,128)(2,1)} %q_hbm.1) | copy-start | bytes 1572868
  2.3 1.0 %copy-start.1 = (bf16[128,2048]{1,0:T(8,128)(2,1)S(1)}, bf16[128,2048]{1,0:T(8,128)(2,1)}, u32[]{:S(2)}) copy-start(bf16[128,2048]{1,0:T(8,128)(2,1)} %o_hbm.1) | copy-start | bytes 1572868
  3.4 1.0 %copy-start.2 = (bf16[128,2048]{1,0:T(8,128)(2,1)S(1)}, bf16[128,2048]{1,0:T(8,128)(2,1)}, u32[]{:S(2)}) copy-start(bf16[128,2048]{1,0:T(8,128)(2,1)} %g_hbm.1) | copy-start | bytes 1572868
  4.4 0.9 %copy-start.3 = (bf16[128,1024]{1,0:T(8,128)(2,1)S(1)}, bf16[128,1024]{1,0:T(8,128)(2,1)}, u32[]{:S(2)}) copy-start(bf16[128,1024]{1,0:T(8,128)(2,1)} %k_hbm.1) | copy-start | bytes 786436
  5.4 0.9 %copy-start.4 = (bf16[128,1024]{1,0:T(8,128)(2,1)S(1)}, bf16[128,1024]{1,0:T(8,128)(2,1)}, u32[]{:S(2)}) copy-start(bf16[128,1024]{1,0:T(8,128)(2,1)} %v_hbm.1) | copy-start | bytes 786436
  6.3 0.9 %copy-start.5 = (s32[65536]{0:T(1024)S(1)}, s32[65536]{0:T(1024)}, u32[]{:S(2)}) copy-start(s32[65536]{0:T(1024)} %param.12) | copy-start | bytes 786436

commit v2 on v1

--- a/solution.py
+++ b/solution.py
@@ -23,9 +23,10 @@
 
 
 def kernel(
-    q_hbm, k_hbm, v_hbm, o_hbm, g_hbm, seg, order,
+    q_hbm, k_hbm, v_hbm, o_hbm, g_hbm, seg_hbm, order_hbm,
     dq_out, dk_out, dv_out,
-    q_all, g_all, k_all, v_all, kt_all, d_all, d_mine, o_rows, g_rows,
+    seg, order, q_all, g_all, k_all, v_all, kt_all, d_all, d_mine, o_rows, g_rows,
+    q_two, g_two, w_all, s_all,
     halo, back, dk_sum, dv_sum, dq_stage, dk_stage, dv_stage, bias,
     load_sem, own_sem, in_send, in_recv, halo_send, halo_recv, back_send, back_recv,
     out_send, out_recv, out_own,
@@ -52,6 +53,8 @@
     loads = [
         pltpu.make_async_copy(o_hbm, o_rows, load_sem.at[0]),
         pltpu.make_async_copy(g_hbm, g_rows, load_sem.at[1]),
+        pltpu.make_async_copy(seg_hbm, seg, load_sem.at[2]),
+        pltpu.make_async_copy(order_hbm, order, load_sem.at[3]),
     ]
     for c in loads:
         c.start()
@@ -102,11 +105,20 @@
             product.T, axis=0, keepdims=True
         )
 
+    mine = h // 4
+    near = [mine * 4 + lax.rem(lax.rem(h, 4) + d, 4) for d in (1, 2, 3)]
+    far = [(1 - mine) * 4 + lax.rem(lax.rem(h, 4) + d, 4) for d in (2, 3, 1, 0)]
     pl.semaphore_wait(barrier, GROUPS + 1)
-    for kind in range(KINDS):
+    for kind in range(3):
         for o in partners:
             send(kind, o).start()
         own(kind).start()
+    for group in (near, far):
+        for kind in (3, 4):
+            for o in group:
+                send(kind, o).start()
+            if group is near:
+                own(kind).start()
 
     slot_half = [order[2 * i], order[2 * i + 1]]
     early = (slot_half[0] > slot_half[1]).astype(jnp.int32)
@@ -133,8 +145,6 @@
                     bias[s, p, r * CHUNK : (r + 1) * CHUNK, :] = jnp.where(
                         visible, 0.0, HIDDEN
                     )
-    dk_sum[...] = jnp.zeros_like(dk_sum)
-    dv_sum[...] = jnp.zeros_like(dv_sum)
 
     for kind in (0, 1):
         for o in partners:
@@ -165,10 +175,9 @@
         kt_all[s, :, :HALF] = before.T
         v_all[s, :HALF, :] = halo[at, 1]
 
-    for kind in (2, 3, 4):
-        for o in partners:
-            arrival(kind, o).wait_recv()
-        own(kind).wait()
+    for o in partners:
+        arrival(2, o).wait_recv()
+    own(2).wait()
 
     def out_piece(kind, target, source):
         if kind == 0:
@@ -188,47 +197,60 @@
         src, dst = out_piece(kind, h, h)
         return pltpu.make_async_copy(src, dst, out_own.at[kind])
 
-    def give(kind, o):
-        @pl.when(o != h)
-        def _():
-            out_remote(kind, o, h, o).start()
-
-        @pl.when(o == h)
-        def _():
-            out_local(kind).start()
-
-    def tile(s, p):
+    def weigh(s, p):
         o = s * 4 + p
-        keys_at = pl.ds(pl.multiple_of(p * CHUNK, CHUNK), WINDOW)
-        keys = k_all[s, keys_at, :]
-        vals = v_all[s, keys_at, :]
-        q_two = jnp.concatenate([q_all[o, :, :HEAD], q_all[o, :, HEAD:]], axis=0)
-        g_two = jnp.concatenate([g_all[o, :, :HEAD], g_all[o, :, HEAD:]], axis=0)
+        window = slice(p * CHUNK, p * CHUNK + WINDOW)
+        at = slice(p * 2 * CHUNK, (p + 1) * 2 * CHUNK)
+        queries = jnp.concatenate([q_all[o, :, :HEAD], q_all[o, :, HEAD:]], axis=0)
+        grads = jnp.concatenate([g_all[o, :, :HEAD], g_all[o, :, HEAD:]], axis=0)
+        q_two[s, at, :] = queries
+        g_two[s, at, :] = grads
         delta = jnp.concatenate([d_all[o, 0:1, :], d_all[o, 1:2, :]], axis=1)
         hide = bias[s, p]
-        scores = lax.dot_general(keys, q_two, NT, preferred_element_type=F32)
+        scores = lax.dot_general(k_all[s, window, :], queries, NT, preferred_element_type=F32)
         scores = scores * (SCALE * LOG2E) + jnp.concatenate([hide, hide], axis=1)
         top = jnp.max(scores, axis=0, keepdims=True)
         terms = jnp.exp2(scores - top)
         weights = terms * (1.0 / jnp.sum(terms, axis=0, keepdims=True))
-        weights_b = weights.astype(BF16)
-        pulls = lax.dot_general(vals, g_two, NT, preferred_element_type=F32)
+        w_all[s, window, at] = weights.astype(BF16)
+        pulls = lax.dot_general(v_all[s, window, :], grads, NT, preferred_element_type=F32)
         score_grads = (weights * (pulls - delta)).astype(BF16)
-        dv_sum[s, keys_at, :] += jnp.dot(weights_b, g_two, preferred_element_type=F32)
-        dk_sum[s, keys_at, :] += jnp.dot(score_grads, q_two, preferred_element_type=F32)
-        dq = jnp.dot(kt_all[s, :, keys_at], score_grads, preferred_element_type=F32) * SCALE
+        s_all[s, window, at] = score_grads
+        dq = jnp.dot(kt_all[s, :, window], score_grads, preferred_element_type=F32) * SCALE
         dq_stage[o, :, :HEAD] = dq[:, :HEAD].T.astype(BF16)
         dq_stage[o, :, HEAD:] = dq[:, HEAD:].T.astype(BF16)
 
-    def step(d, carry):
-        p = lax.rem(h + 1 + d, 4)
-        for s in range(2):
-            tile(s, p)
-        for s in range(2):
-            give(0, s * 4 + p)
-        return carry
-
-    lax.fori_loop(0, 4, step, 0)
+    def key_terms(s, c):
+        rows = slice(c * CHUNK, (c + 1) * CHUNK)
+        at = slice(max(0, c - 4) * 2 * CHUNK, (min(3, c) + 1) * 2 * CHUNK)
+        dv_sum[s, rows, :] = jnp.dot(
+            w_all[s, rows, at], g_two[s, at, :], preferred_element_type=F32
+        )
+        dk_sum[s, rows, :] = jnp.dot(
+            s_all[s, rows, at], q_two[s, at, :], preferred_element_type=F32
+        )
+
+    for kind in (3, 4):
+        for o in near:
+            arrival(kind, o).wait_recv()
+        own(kind).wait()
+    for p in range(4):
+        weigh(mine, p)
+    for o in near:
+        out_remote(0, o, h, o).start()
+    out_local(0).start()
+    for c in range(8):
+        key_terms(mine, c)
+
+    for kind in (3, 4):
+        for o in far:
+            arrival(kind, o).wait_recv()
+    for p in range(4):
+        weigh(1 - mine, p)
+        o = (1 - mine) * 4 + p
+        out_remote(0, o, h, o).start()
+    for c in range(8):
+        key_terms(1 - mine, c)
 
     for n, slot in ((2, early), (3, late)):
         back[n, 0] = dk_sum[slot, :HALF, :].astype(BF16)
@@ -276,9 +298,7 @@
 
 def local(queries, keys, values, outputs, out_grads, segment_ids, block_order):
     rows = queries.shape[0]
-    hbm = pl.BlockSpec(memory_space=pl.ANY)
-    vmem = pl.BlockSpec(memory_space=pltpu.VMEM)
-    smem = pl.BlockSpec(memory_space=pltpu.SMEM)
+    hbm = pl.BlockSpec(memory_space=pltpu.HBM)
     dma = pltpu.SemaphoreType.DMA
     return pl.pallas_call(
         kernel,
@@ -287,9 +307,11 @@
             jax.ShapeDtypeStruct((rows, keys.shape[1]), BF16),
             jax.ShapeDtypeStruct((rows, values.shape[1]), BF16),
         ],
-        in_specs=[hbm] * 5 + [vmem, smem],
+        in_specs=[hbm] * 7,
         out_specs=[hbm] * 3,
         scratch_shapes=[
+            pltpu.VMEM((segment_ids.shape[0] // CHUNK, CHUNK), jnp.int32),
+            pltpu.SMEM(block_order.shape, jnp.int32),
             pltpu.VMEM((GROUPS, CHUNK, 2 * HEAD), BF16),
             pltpu.VMEM((GROUPS, CHUNK, 2 * HEAD), BF16),
             pltpu.VMEM((2, 2 * HALF, HEAD), BF16),
@@ -299,6 +321,10 @@
             pltpu.VMEM((GROUPS, 8, CHUNK), F32),
             pltpu.VMEM((CHUNK, 2 * GROUPS * HEAD), BF16),
             pltpu.VMEM((CHUNK, 2 * GROUPS * HEAD), BF16),
+            pltpu.VMEM((2, 2 * HALF, HEAD), BF16),
+            pltpu.VMEM((2, 2 * HALF, HEAD), BF16),
+            pltpu.VMEM((2, 2 * HALF, 2 * HALF), BF16),
+            pltpu.VMEM((2, 2 * HALF, 2 * HALF), BF16),
             pltpu.VMEM((4, 2, HALF, HEAD), BF16),
             pltpu.VMEM((4, 2, HALF, HEAD), BF16),
             pltpu.VMEM((2, 2 * HALF, HEAD), F32),
@@ -307,7 +333,7 @@
             pltpu.VMEM((GROUPS, CHUNK, HEAD), BF16),
             pltpu.VMEM((GROUPS, CHUNK, HEAD), BF16),
             pltpu.VMEM((2, 4, WINDOW, CHUNK), F32),
-            dma((2,)),
+            dma((4,)),
             dma((KINDS,)),
             dma((KINDS, GROUPS)),
             dma((KINDS, GROUPS)),
@@ -320,7 +346,7 @@
             dma((3,)),
         ],
         compiler_params=pltpu.CompilerParams(
-            collective_id=0, has_side_effects=True, vmem_limit_bytes=40 * 1024 * 1024
+            collective_id=0, has_side_effects=True, vmem_limit_bytes=60 * 1024 * 1024
         ),
         name="attention_backward",
     )(

time: 66.1 us -> 59.6 us (0.902)
  the two profiles are of different devices: /device:TPU:64 before, /device:TPU:2 now
where the time goes in v2:
time: 59.6 us; the launch traced here: 59.4 us
  Pallas kernels  55.1 us (92%)
  local copies, waits for them, and re-layouts  3.67 us (6%)
  between operations  0.65 us (1%)
    pallas_call x1, Pallas kernels, local(): pl.pallas_call(kernel, out_shape=[jax.ShapeDtypeStruct((rows, queries.sha...  55.1 us
    unnamed x7, local copies, waits for them, and re-layouts  3.67 us

profile of v2, /device:TPU:2, one launch (start us, length us, event | category | flops | bytes accessed | tf_op | source)
XLA Modules:
  0.0 59.4 jit_solution(7704785140728570532)
XLA Ops:
  0.6 55.1 %attention_backward.1 = (bf16[128,2048]{1,0:T(8,128)(2,1)}, bf16[128,1024]{1,0:T(8,128)(2,1)}, bf16[128,1024]{1,0:T(8,128)(2,1)}) custom-call(bf16[128,2048]{1,0:T(8,128)(2,1)} %q_hbm.1, bf16[128,1024]{1,0:T(8,128)(2,1)} %k_hbm.1, bf16[128,1024]{1,0:T(8,128)(2,1)} %v_hbm.1, bf16[128,2048]{1,0:T(8,128)(2,1)} %o_hbm.1, bf16[128,2048]{1,0:T(8,128)(2,1)} %g_hbm.1, ...), custom_call_target="tpu_custom_call" | custom-call | tf_op jit(solution)/shard_map/attention_backward/pallas_call | solution.py:303
  55.7 0.0 copy-start.1
  55.7 1.9 %copy.13 = bf16[128,2048]{1,0:T(8,128)(2,1)} copy(bf16[128,2048]{1,0:T(8,128)(2,1)} %get-tuple-element.6) | data formatting | bytes 1048576
  57.7 0.0 copy-done.1
  57.7 0.0 copy-start
  57.7 0.7 %copy.14 = bf16[128,1024]{1,0:T(8,128)(2,1)} copy(bf16[128,1024]{1,0:T(8,128)(2,1)S(1)} %copy-done.1) | data formatting | bytes 524288
  58.4 0.3 copy-done
  58.7 0.7 %copy.15 = bf16[128,1024]{1,0:T(8,128)(2,1)} copy(bf16[128,1024]{1,0:T(8,128)(2,1)S(1)} %copy-done) | data formatting | bytes 524288
Async XLA Ops:
  55.7 1.9 %copy-start.1 = (bf16[128,1024]{1,0:T(8,128)(2,1)S(1)}, bf16[128,1024]{1,0:T(8,128)(2,1)}, u32[]{:S(2)}) copy-start(bf16[128,1024]{1,0:T(8,128)(2,1)} %get-tuple-element.7) | copy-start | bytes 786436
  57.7 1.0 %copy-start = (bf16[128,1024]{1,0:T(8,128)(2,1)S(1)}, bf16[128,1024]{1,0:T(8,128)(2,1)}, u32[]{:S(2)}) copy-start(bf16[128,1024]{1,0:T(8,128)(2,1)} %get-tuple-element.8) | copy-start | bytes 786436

commit v3 on v2

--- a/solution.py
+++ b/solution.py
@@ -35,8 +35,10 @@
     h = lax.axis_index("head")
     blocks = lax.axis_size("blk")
     x, z = h // 2, h % 2
-    above = lax.rem(i + 1, blocks)
-    below = lax.rem(i + blocks - 1, blocks)
+    has_above = i < blocks - 1
+    has_below = i > 0
+    above = jnp.minimum(i + 1, blocks - 1)
+    below = jnp.maximum(i - 1, 0)
     partners = [
         lax.rem(x + dx, 4) * 2 + lax.rem(z + dz, 2)
         for dx in (2, 1, 3, 0)
@@ -47,8 +49,10 @@
     barrier = pltpu.get_barrier_semaphore()
     for o in partners:
         pl.semaphore_signal(barrier, inc=1, device_id=(i, o), device_id_type=MESH)
-    for b in (above, below):
-        pl.semaphore_signal(barrier, inc=1, device_id=(b, h), device_id_type=MESH)
+    for there, b in ((has_above, above), (has_below, below)):
+        @pl.when(there)
+        def _():
+            pl.semaphore_signal(barrier, inc=1, device_id=(b, h), device_id_type=MESH)
 
     loads = [
         pltpu.make_async_copy(o_hbm, o_rows, load_sem.at[0]),
@@ -108,11 +112,14 @@
     mine = h // 4
     near = [mine * 4 + lax.rem(lax.rem(h, 4) + d, 4) for d in (1, 2, 3)]
     far = [(1 - mine) * 4 + lax.rem(lax.rem(h, 4) + d, 4) for d in (2, 3, 1, 0)]
-    pl.semaphore_wait(barrier, GROUPS + 1)
+    pl.semaphore_wait(
+        barrier, GROUPS - 1 + has_above.astype(jnp.int32) + has_below.astype(jnp.int32)
+    )
     for kind in range(3):
         for o in partners:
             send(kind, o).start()
         own(kind).start()
+
     for group in (near, far):
         for kind in (3, 4):
             for o in group:
@@ -162,14 +169,14 @@
         halo.at[3], halo.at[1], halo_send.at[1], halo_recv.at[1],
         device_id=(below, h), device_id_type=MESH,
     )
-    halo_up.start()
-    halo_down.start()
+    pl.when(has_above)(lambda: halo_up.start())
+    pl.when(has_below)(lambda: halo_down.start())
     for s in range(2):
         kt_all[s, :, HALF:] = k_all[s, HALF:, :].T
-    halo_up.wait_recv()
-    halo_down.wait_recv()
+    pl.when(has_below)(lambda: halo_up.wait_recv())
+    pl.when(has_above)(lambda: halo_down.wait_recv())
     for s in range(2):
-        at = jnp.where(is_early[s], 0, jnp.where(i == blocks - 1, 2, 1))
+        at = jnp.where(is_early[s], jnp.where(has_below, 0, 2), jnp.where(has_above, 1, 2))
         before = halo[at, 0]
         k_all[s, :HALF, :] = before
         kt_all[s, :, :HALF] = before.T
@@ -247,9 +254,7 @@
             arrival(kind, o).wait_recv()
     for p in range(4):
         weigh(1 - mine, p)
-        o = (1 - mine) * 4 + p
-        out_remote(0, o, h, o).start()
-    for c in range(8):
+    for c in range(4):
         key_terms(1 - mine, c)
 
     for n, slot in ((2, early), (3, late)):
@@ -263,13 +268,17 @@
         back.at[3], back.at[0], back_send.at[1], back_recv.at[1],
         device_id=(above, h), device_id_type=MESH,
     )
-    back_down.start()
-    back_up.start()
-    back_down.wait_recv()
-    back_up.wait_recv()
+    pl.when(has_below)(lambda: back_down.start())
+    pl.when(has_above)(lambda: back_up.start())
+    for o in far:
+        out_remote(0, o, h, o).start()
+    for c in range(4, 8):
+        key_terms(1 - mine, c)
+    pl.when(has_above)(lambda: back_down.wait_recv())
+    pl.when(has_below)(lambda: back_up.wait_recv())
     for s in range(2):
-        at = jnp.where(is_early[s], jnp.where(i == blocks - 1, 3, 1), 0)
-        nothing = jnp.logical_and(jnp.logical_not(is_early[s]), i == 0)
+        at = jnp.where(is_early[s], jnp.where(has_above, 1, 3), jnp.where(has_below, 0, 2))
+        nothing = jnp.logical_not(jnp.logical_or(is_early[s], has_below))
         for p in range(4):
             own_at = slice(HALF + p * CHUNK, HALF + (p + 1) * CHUNK)
             rows = slice(p * CHUNK, (p + 1) * CHUNK)
@@ -282,10 +291,10 @@
             out_remote(kind, o, h, o).start()
         out_local(kind).start()
 
-    halo_up.wait_send()
-    halo_down.wait_send()
-    back_down.wait_send()
-    back_up.wait_send()
+    pl.when(has_above)(lambda: halo_up.wait_send())
+    pl.when(has_below)(lambda: halo_down.wait_send())
+    pl.when(has_below)(lambda: back_down.wait_send())
+    pl.when(has_above)(lambda: back_up.wait_send())
     for kind in range(KINDS):
         for o in partners:
             send(kind, o).wait_send()
@@ -296,17 +305,19 @@
         out_local(kind).wait()
 
 
+def settle(dq_in, dk_in, dv_in, dq_out, dk_out, dv_out):
+    dq_out[...] = dq_in[...]
+    dk_out[...] = dk_in[...]
+    dv_out[...] = dv_in[...]
+
+
 def local(queries, keys, values, outputs, out_grads, segment_ids, block_order):
-    rows = queries.shape[0]
     hbm = pl.BlockSpec(memory_space=pltpu.HBM)
     dma = pltpu.SemaphoreType.DMA
-    return pl.pallas_call(
+    shapes = [jax.ShapeDtypeStruct(a.shape, BF16) for a in (queries, keys, values)]
+    grads = pl.pallas_call(
         kernel,
-        out_shape=[
-            jax.ShapeDtypeStruct((rows, queries.shape[1]), BF16),
-            jax.ShapeDtypeStruct((rows, keys.shape[1]), BF16),
-            jax.ShapeDtypeStruct((rows, values.shape[1]), BF16),
-        ],
+        out_shape=shapes,
         in_specs=[hbm] * 7,
         out_specs=[hbm] * 3,
         scratch_shapes=[
@@ -353,6 +364,12 @@
         queries, keys, values, outputs, out_grads,
         segment_ids.reshape(-1, CHUNK), block_order,
     )
+    return pl.pallas_call(
+        settle,
+        out_shape=shapes,
+        compiler_params=pltpu.CompilerParams(vmem_limit_bytes=60 * 1024 * 1024),
+        name="settle",
+    )(*grads)
 
 
 def solution(mesh):

time: 59.6 us -> 53.9 us (0.904)
  the two profiles are of different devices: /device:TPU:2 before, /device:TPU:57 now
where the time goes in v3:
time: 53.9 us; the launch traced here: 53.7 us
  Pallas kernels  53.1 us (99%)
  between operations  0.64 us (1%)
    pallas_call x1, Pallas kernels, local(): pl.pallas_call(kernel, out_shape=shapes, in_specs=[hbm] * 7, out_specs=[h...  50.9 us
    pallas_call x1, Pallas kernels, local(): pl.pallas_call(settle, out_shape=shapes, compiler_params=pltpu.CompilerPa...  2.17 us

profile of v3, /device:TPU:57, one launch (start us, length us, event | category | flops | bytes accessed | tf_op | source)
XLA Modules:
  0.0 53.7 jit_solution(5438940711984894354)
XLA Ops:
  0.6 50.9 %attention_backward.1 = (bf16[128,2048]{1,0:T(8,128)(2,1)}, bf16[128,1024]{1,0:T(8,128)(2,1)}, bf16[128,1024]{1,0:T(8,128)(2,1)}) custom-call(bf16[128,2048]{1,0:T(8,128)(2,1)} %q_hbm.1, bf16[128,1024]{1,0:T(8,128)(2,1)} %k_hbm.1, bf16[128,1024]{1,0:T(8,128)(2,1)} %v_hbm.1, bf16[128,2048]{1,0:T(8,128)(2,1)} %o_hbm.1, bf16[128,2048]{1,0:T(8,128)(2,1)} %g_hbm.1, ...), custom_call_target="tpu_custom_call" | custom-call | tf_op jit(solution)/shard_map/attention_backward/pallas_call | solution.py:318
  51.5 2.2 %settle.1 = (bf16[128,2048]{1,0:T(8,128)(2,1)}, bf16[128,1024]{1,0:T(8,128)(2,1)}, bf16[128,1024]{1,0:T(8,128)(2,1)}) custom-call(bf16[128,2048]{1,0:T(8,128)(2,1)} %get-tuple-element.6.dq_in, bf16[128,1024]{1,0:T(8,128)(2,1)} %get-tuple-element.7.dk_in, bf16[128,1024]{1,0:T(8,128)(2,1)} %get-tuple-element.8.dv_in), custom_call_target="tpu_custom_call" | custom-call | tf_op jit(solution)/shard_map/settle/pallas_call | solution.py:367

commit v4 on v3

--- a/solution.py
+++ b/solution.py
@@ -27,7 +27,7 @@
     dq_out, dk_out, dv_out,
     seg, order, q_all, g_all, k_all, v_all, kt_all, d_all, d_mine, o_rows, g_rows,
     q_two, g_two, w_all, s_all,
-    halo, back, dk_sum, dv_sum, dq_stage, dk_stage, dv_stage, bias,
+    halo, back_k, back_v, dk_sum, dv_sum, dq_stage, dk_stage, dv_stage, bias,
     load_sem, own_sem, in_send, in_recv, halo_send, halo_recv, back_send, back_recv,
     out_send, out_recv, out_own,
 ):
@@ -258,43 +258,47 @@
         key_terms(1 - mine, c)
 
     for n, slot in ((2, early), (3, late)):
-        back[n, 0] = dk_sum[slot, :HALF, :].astype(BF16)
-        back[n, 1] = dv_sum[slot, :HALF, :].astype(BF16)
-    back_down = pltpu.make_async_remote_copy(
-        back.at[2], back.at[1], back_send.at[0], back_recv.at[0],
-        device_id=(below, h), device_id_type=MESH,
-    )
-    back_up = pltpu.make_async_remote_copy(
-        back.at[3], back.at[0], back_send.at[1], back_recv.at[1],
-        device_id=(above, h), device_id_type=MESH,
-    )
-    pl.when(has_below)(lambda: back_down.start())
-    pl.when(has_above)(lambda: back_up.start())
+        back_k[n] = dk_sum[slot, :HALF, :].astype(BF16)
+        back_v[n] = dv_sum[slot, :HALF, :].astype(BF16)
+    back_down, back_up = {}, {}
+    for n, back in ((1, back_v), (0, back_k)):
+        back_down[n] = pltpu.make_async_remote_copy(
+            back.at[2], back.at[1], back_send.at[0, n], back_recv.at[0, n],
+            device_id=(below, h), device_id_type=MESH,
+        )
+        back_up[n] = pltpu.make_async_remote_copy(
+            back.at[3], back.at[0], back_send.at[1, n], back_recv.at[1, n],
+            device_id=(above, h), device_id_type=MESH,
+        )
+        pl.when(has_below)(lambda: back_down[n].start())
+        pl.when(has_above)(lambda: back_up[n].start())
     for o in far:
         out_remote(0, o, h, o).start()
     for c in range(4, 8):
         key_terms(1 - mine, c)
-    pl.when(has_above)(lambda: back_down.wait_recv())
-    pl.when(has_below)(lambda: back_up.wait_recv())
-    for s in range(2):
-        at = jnp.where(is_early[s], jnp.where(has_above, 1, 3), jnp.where(has_below, 0, 2))
-        nothing = jnp.logical_not(jnp.logical_or(is_early[s], has_below))
-        for p in range(4):
-            own_at = slice(HALF + p * CHUNK, HALF + (p + 1) * CHUNK)
-            rows = slice(p * CHUNK, (p + 1) * CHUNK)
-            dk_more = jnp.where(nothing, 0.0, back[at, 0, rows, :].astype(F32))
-            dv_more = jnp.where(nothing, 0.0, back[at, 1, rows, :].astype(F32))
-            dk_stage[s * 4 + p] = ((dk_sum[s, own_at, :] + dk_more) * SCALE).astype(BF16)
-            dv_stage[s * 4 + p] = (dv_sum[s, own_at, :] + dv_more).astype(BF16)
-    for kind in (1, 2):
+    for n, back, total, stage, scale in (
+        (1, back_v, dv_sum, dv_stage, 1.0),
+        (0, back_k, dk_sum, dk_stage, SCALE),
+    ):
+        pl.when(has_above)(lambda: back_down[n].wait_recv())
+        pl.when(has_below)(lambda: back_up[n].wait_recv())
+        for s in range(2):
+            at = jnp.where(is_early[s], jnp.where(has_above, 1, 3), jnp.where(has_below, 0, 2))
+            nothing = jnp.logical_not(jnp.logical_or(is_early[s], has_below))
+            for p in range(4):
+                own_at = slice(HALF + p * CHUNK, HALF + (p + 1) * CHUNK)
+                rows = slice(p * CHUNK, (p + 1) * CHUNK)
+                more = jnp.where(nothing, 0.0, back[at, rows, :].astype(F32))
+                stage[s * 4 + p] = ((total[s, own_at, :] + more) * scale).astype(BF16)
         for o in partners:
-            out_remote(kind, o, h, o).start()
-        out_local(kind).start()
+            out_remote(2 if n else 1, o, h, o).start()
+        out_local(2 if n else 1).start()
 
     pl.when(has_above)(lambda: halo_up.wait_send())
     pl.when(has_below)(lambda: halo_down.wait_send())
-    pl.when(has_below)(lambda: back_down.wait_send())
-    pl.when(has_above)(lambda: back_up.wait_send())
+    for n in (0, 1):
+        pl.when(has_below)(lambda: back_down[n].wait_send())
+        pl.when(has_above)(lambda: back_up[n].wait_send())
     for kind in range(KINDS):
         for o in partners:
             send(kind, o).wait_send()
@@ -305,10 +309,21 @@
         out_local(kind).wait()
 
 
-def settle(dq_in, dk_in, dv_in, dq_out, dk_out, dv_out):
-    dq_out[...] = dq_in[...]
-    dk_out[...] = dk_in[...]
-    dv_out[...] = dv_in[...]
+def settle(dq_in, dk_in, dv_in, dq_out, dk_out, dv_out, dq_mid, dk_mid, dv_mid, sem):
+    trios = []
+    for a, m, b in ((dq_in, dq_mid, dq_out), (dk_in, dk_mid, dk_out), (dv_in, dv_mid, dv_out)):
+        for part in range(2):
+            rows = pl.ds(part * 64, 64)
+            trios.append((a.at[rows, :], m.at[rows, :], b.at[rows, :]))
+    ins = [pltpu.make_async_copy(a, m, sem.at[0, n]) for n, (a, m, _) in enumerate(trios)]
+    outs = [pltpu.make_async_copy(m, b, sem.at[1, n]) for n, (_, m, b) in enumerate(trios)]
+    for c in ins:
+        c.start()
+    for c, d in zip(ins, outs):
+        c.wait()
+        d.start()
+    for d in outs:
+        d.wait()
 
 
 def local(queries, keys, values, outputs, out_grads, segment_ids, block_order):
@@ -337,7 +352,8 @@
             pltpu.VMEM((2, 2 * HALF, 2 * HALF), BF16),
             pltpu.VMEM((2, 2 * HALF, 2 * HALF), BF16),
             pltpu.VMEM((4, 2, HALF, HEAD), BF16),
-            pltpu.VMEM((4, 2, HALF, HEAD), BF16),
+            pltpu.VMEM((4, HALF, HEAD), BF16),
+            pltpu.VMEM((4, HALF, HEAD), BF16),
             pltpu.VMEM((2, 2 * HALF, HEAD), F32),
             pltpu.VMEM((2, 2 * HALF, HEAD), F32),
             pltpu.VMEM((GROUPS, CHUNK, 2 * HEAD), BF16),
@@ -350,8 +366,8 @@
             dma((KINDS, GROUPS)),
             dma((2,)),
             dma((2,)),
-            dma((2,)),
-            dma((2,)),
+            dma((2, 2)),
+            dma((2, 2)),
             dma((3, GROUPS)),
             dma((3, GROUPS)),
             dma((3,)),
@@ -367,6 +383,9 @@
     return pl.pallas_call(
         settle,
         out_shape=shapes,
+        in_specs=[hbm] * 3,
+        out_specs=[hbm] * 3,
+        scratch_shapes=[pltpu.VMEM(a.shape, BF16) for a in shapes] + [dma((2, 6))],
         compiler_params=pltpu.CompilerParams(vmem_limit_bytes=60 * 1024 * 1024),
         name="settle",
     )(*grads)

time: 53.9 us -> 52.6 us (0.976)
  Pallas kernels: 53.1 us -> 51.5 us
    pallas_call x1, Pallas kernels: 50.9 us -> 49.5 us  [local(): pl.pallas_call(kernel, out_shape=shapes, in_specs=[hbm] * 7, out_specs=[h...]
where the time goes in v4:
time: 52.6 us; the launch traced here: 52.1 us
  Pallas kernels  51.5 us (98%)
  between operations  0.64 us (1%)
    pallas_call x1, Pallas kernels, local(): pl.pallas_call(kernel, out_shape=shapes, in_specs=[hbm] * 7, out_specs=[h...  49.5 us
    pallas_call x1, Pallas kernels, local(): pl.pallas_call(settle, out_shape=shapes, in_specs=[hbm] * 3, out_specs=[h...  2.01 us

profile of v4, /device:TPU:57, one launch (start us, length us, event | category | flops | bytes accessed | tf_op | source)
XLA Modules:
  0.0 52.1 jit_solution(10204927629099173379)
XLA Ops:
  0.6 49.5 %attention_backward.1 = (bf16[128,2048]{1,0:T(8,128)(2,1)}, bf16[128,1024]{1,0:T(8,128)(2,1)}, bf16[128,1024]{1,0:T(8,128)(2,1)}) custom-call(bf16[128,2048]{1,0:T(8,128)(2,1)} %q_hbm.1, bf16[128,1024]{1,0:T(8,128)(2,1)} %k_hbm.1, bf16[128,1024]{1,0:T(8,128)(2,1)} %v_hbm.1, bf16[128,2048]{1,0:T(8,128)(2,1)} %o_hbm.1, bf16[128,2048]{1,0:T(8,128)(2,1)} %g_hbm.1, ...), custom_call_target="tpu_custom_call" | custom-call | tf_op jit(solution)/shard_map/attention_backward/pallas_call | solution.py:333
  50.1 2.0 %settle.1 = (bf16[128,2048]{1,0:T(8,128)(2,1)}, bf16[128,1024]{1,0:T(8,128)(2,1)}, bf16[128,1024]{1,0:T(8,128)(2,1)}) custom-call(bf16[128,2048]{1,0:T(8,128)(2,1)} %get-tuple-element.6.dq_in, bf16[128,1024]{1,0:T(8,128)(2,1)} %get-tuple-element.7.dk_in, bf16[128,1024]{1,0:T(8,128)(2,1)} %get-tuple-element.8.dv_in), custom_call_target="tpu_custom_call" | custom-call | tf_op jit(solution)/shard_map/settle/pallas_call | solution.py:383

commit v5 on v4

--- a/solution.py
+++ b/solution.py
@@ -27,7 +27,7 @@
     dq_out, dk_out, dv_out,
     seg, order, q_all, g_all, k_all, v_all, kt_all, d_all, d_mine, o_rows, g_rows,
     q_two, g_two, w_all, s_all,
-    halo, back_k, back_v, dk_sum, dv_sum, dq_stage, dk_stage, dv_stage, bias,
+    halo_k, halo_v, back_k, back_v, dk_sum, dv_sum, dq_stage, dk_stage, dv_stage, bias,
     load_sem, own_sem, in_send, in_recv, halo_send, halo_recv, back_send, back_recv,
     out_send, out_recv, out_own,
 ):
@@ -153,34 +153,35 @@
                         visible, 0.0, HIDDEN
                     )
 
-    for kind in (0, 1):
+    late = 1 - early
+    halo_up, halo_down = {}, {}
+    for n, halo, rows in ((0, halo_k, k_all), (1, halo_v, v_all)):
         for o in partners:
-            arrival(kind, o).wait_recv()
-        own(kind).wait()
-    late = 1 - early
-    for n, slot in ((2, early), (3, late)):
-        halo[n, 0] = k_all[slot, HALF:, :]
-        halo[n, 1] = v_all[slot, HALF:, :]
-    halo_up = pltpu.make_async_remote_copy(
-        halo.at[2], halo.at[0], halo_send.at[0], halo_recv.at[0],
-        device_id=(above, h), device_id_type=MESH,
-    )
-    halo_down = pltpu.make_async_remote_copy(
-        halo.at[3], halo.at[1], halo_send.at[1], halo_recv.at[1],
-        device_id=(below, h), device_id_type=MESH,
-    )
-    pl.when(has_above)(lambda: halo_up.start())
-    pl.when(has_below)(lambda: halo_down.start())
+            arrival(n, o).wait_recv()
+        own(n).wait()
+        for m, slot in ((2, early), (3, late)):
+            halo[m] = rows[slot, HALF:, :]
+        halo_up[n] = pltpu.make_async_remote_copy(
+            halo.at[2], halo.at[0], halo_send.at[0, n], halo_recv.at[0, n],
+            device_id=(above, h), device_id_type=MESH,
+        )
+        halo_down[n] = pltpu.make_async_remote_copy(
+            halo.at[3], halo.at[1], halo_send.at[1, n], halo_recv.at[1, n],
+            device_id=(below, h), device_id_type=MESH,
+        )
+        pl.when(has_above)(lambda: halo_up[n].start())
+        pl.when(has_below)(lambda: halo_down[n].start())
     for s in range(2):
         kt_all[s, :, HALF:] = k_all[s, HALF:, :].T
-    pl.when(has_below)(lambda: halo_up.wait_recv())
-    pl.when(has_above)(lambda: halo_down.wait_recv())
-    for s in range(2):
-        at = jnp.where(is_early[s], jnp.where(has_below, 0, 2), jnp.where(has_above, 1, 2))
-        before = halo[at, 0]
-        k_all[s, :HALF, :] = before
-        kt_all[s, :, :HALF] = before.T
-        v_all[s, :HALF, :] = halo[at, 1]
+    for n, halo, rows in ((0, halo_k, k_all), (1, halo_v, v_all)):
+        pl.when(has_below)(lambda: halo_up[n].wait_recv())
+        pl.when(has_above)(lambda: halo_down[n].wait_recv())
+        for s in range(2):
+            at = jnp.where(is_early[s], jnp.where(has_below, 0, 2), jnp.where(has_above, 1, 2))
+            before = halo[at]
+            rows[s, :HALF, :] = before
+            if n == 0:
+                kt_all[s, :, :HALF] = before.T
 
     for o in partners:
         arrival(2, o).wait_recv()
@@ -227,14 +228,12 @@
         dq_stage[o, :, :HEAD] = dq[:, :HEAD].T.astype(BF16)
         dq_stage[o, :, HEAD:] = dq[:, HEAD:].T.astype(BF16)
 
-    def key_terms(s, c):
+    def key_terms(n, s, c):
+        total, parts, rows_two = ((dk_sum, s_all, q_two), (dv_sum, w_all, g_two))[n]
         rows = slice(c * CHUNK, (c + 1) * CHUNK)
         at = slice(max(0, c - 4) * 2 * CHUNK, (min(3, c) + 1) * 2 * CHUNK)
-        dv_sum[s, rows, :] = jnp.dot(
-            w_all[s, rows, at], g_two[s, at, :], preferred_element_type=F32
-        )
-        dk_sum[s, rows, :] = jnp.dot(
-            s_all[s, rows, at], q_two[s, at, :], preferred_element_type=F32
+        total[s, rows, :] = jnp.dot(
+            parts[s, rows, at], rows_two[s, at, :], preferred_element_type=F32
         )
 
     for kind in (3, 4):
@@ -246,22 +245,21 @@
     for o in near:
         out_remote(0, o, h, o).start()
     out_local(0).start()
-    for c in range(8):
-        key_terms(mine, c)
+    for n in (1, 0):
+        for c in range(8):
+            key_terms(n, mine, c)
 
     for kind in (3, 4):
         for o in far:
             arrival(kind, o).wait_recv()
     for p in range(4):
         weigh(1 - mine, p)
-    for c in range(4):
-        key_terms(1 - mine, c)
-
-    for n, slot in ((2, early), (3, late)):
-        back_k[n] = dk_sum[slot, :HALF, :].astype(BF16)
-        back_v[n] = dv_sum[slot, :HALF, :].astype(BF16)
     back_down, back_up = {}, {}
-    for n, back in ((1, back_v), (0, back_k)):
+    for n, back, total in ((1, back_v, dv_sum), (0, back_k, dk_sum)):
+        for c in range(4):
+            key_terms(n, 1 - mine, c)
+        for m, slot in ((2, early), (3, late)):
+            back[m] = total[slot, :HALF, :].astype(BF16)
         back_down[n] = pltpu.make_async_remote_copy(
             back.at[2], back.at[1], back_send.at[0, n], back_recv.at[0, n],
             device_id=(below, h), device_id_type=MESH,
@@ -274,8 +272,9 @@
         pl.when(has_above)(lambda: back_up[n].start())
     for o in far:
         out_remote(0, o, h, o).start()
-    for c in range(4, 8):
-        key_terms(1 - mine, c)
+    for n in (1, 0):
+        for c in range(4, 8):
+            key_terms(n, 1 - mine, c)
     for n, back, total, stage, scale in (
         (1, back_v, dv_sum, dv_stage, 1.0),
         (0, back_k, dk_sum, dk_stage, SCALE),
@@ -294,9 +293,9 @@
             out_remote(2 if n else 1, o, h, o).start()
         out_local(2 if n else 1).start()
 
-    pl.when(has_above)(lambda: halo_up.wait_send())
-    pl.when(has_below)(lambda: halo_down.wait_send())
     for n in (0, 1):
+        pl.when(has_above)(lambda: halo_up[n].wait_send())
+        pl.when(has_below)(lambda: halo_down[n].wait_send())
         pl.when(has_below)(lambda: back_down[n].wait_send())
         pl.when(has_above)(lambda: back_up[n].wait_send())
     for kind in range(KINDS):
@@ -351,7 +350,8 @@
             pltpu.VMEM((2, 2 * HALF, HEAD), BF16),
             pltpu.VMEM((2, 2 * HALF, 2 * HALF), BF16),
             pltpu.VMEM((2, 2 * HALF, 2 * HALF), BF16),
-            pltpu.VMEM((4, 2, HALF, HEAD), BF16),
+            pltpu.VMEM((4, HALF, HEAD), BF16),
+            pltpu.VMEM((4, HALF, HEAD), BF16),
             pltpu.VMEM((4, HALF, HEAD), BF16),
             pltpu.VMEM((4, HALF, HEAD), BF16),
             pltpu.VMEM((2, 2 * HALF, HEAD), F32),
@@ -364,8 +364,8 @@
             dma((KINDS,)),
             dma((KINDS, GROUPS)),
             dma((KINDS, GROUPS)),
-            dma((2,)),
-            dma((2,)),
+            dma((2, 2)),
+            dma((2, 2)),
             dma((2, 2)),
             dma((2, 2)),
             dma((3, GROUPS)),

time: 52.6 us -> 52.5 us (level)
  no operation moved by 1% of the time
where the time goes in v5:
time: 52.5 us; the launch traced here: 52 us
  Pallas kernels  51.4 us (98%)
  between operations  0.64 us (1%)
    pallas_call x1, Pallas kernels, local(): pl.pallas_call(kernel, out_shape=shapes, in_specs=[hbm] * 7, out_specs=[h...  49.3 us
    pallas_call x1, Pallas kernels, local(): pl.pallas_call(settle, out_shape=shapes, in_specs=[hbm] * 3, out_specs=[h...  2.01 us

profile of v5, /device:TPU:57, one launch (start us, length us, event | category | flops | bytes accessed | tf_op | source)
XLA Modules:
  0.0 52.0 jit_solution(11018517859460663511)
XLA Ops:
  0.6 49.3 %attention_backward.1 = (bf16[128,2048]{1,0:T(8,128)(2,1)}, bf16[128,1024]{1,0:T(8,128)(2,1)}, bf16[128,1024]{1,0:T(8,128)(2,1)}) custom-call(bf16[128,2048]{1,0:T(8,128)(2,1)} %q_hbm.1, bf16[128,1024]{1,0:T(8,128)(2,1)} %k_hbm.1, bf16[128,1024]{1,0:T(8,128)(2,1)} %v_hbm.1, bf16[128,2048]{1,0:T(8,128)(2,1)} %o_hbm.1, bf16[128,2048]{1,0:T(8,128)(2,1)} %g_hbm.1, ...), custom_call_target="tpu_custom_call" | custom-call | tf_op jit(solution)/shard_map/attention_backward/pallas_call | solution.py:332
  50.0 2.0 %settle.1 = (bf16[128,2048]{1,0:T(8,128)(2,1)}, bf16[128,1024]{1,0:T(8,128)(2,1)}, bf16[128,1024]{1,0:T(8,128)(2,1)}) custom-call(bf16[128,2048]{1,0:T(8,128)(2,1)} %get-tuple-element.6.dq_in, bf16[128,1024]{1,0:T(8,128)(2,1)} %get-tuple-element.7.dk_in, bf16[128,1024]{1,0:T(8,128)(2,1)} %get-tuple-element.8.dv_in), custom_call_target="tpu_custom_call" | custom-call | tf_op jit(solution)/shard_map/settle/pallas_call | solution.py:383
